TPU v7x, 32 devices: a whole 2x2x4 slice. The times are simulated.
32 devices in a mesh: patch: 8 (over z, y), fsdp: 4 (over x, core).
Axes of the slice: x: 2, y: 2, z: 4, core: 2. Of those that a mesh axis runs over, the one named last changes fastest.
Arguments:
- observed: bfloat16 [16384, 256], P(('patch', 'fsdp')), may hold values from -6 to 6
- route: int32 [16384, 1], P(('patch', 'fsdp')), may hold values from 0 to 7, as said below
- grid: bfloat16 [4096, 2048], P(('patch', 'fsdp'))
- gain: float32 [2048], replicated, may hold values from 0.5 to 1.5
- query_weight: bfloat16 [2048, 2048], P(None, 'fsdp'), may hold values from -0.125 to 0.125
- key_weight: bfloat16 [256, 2048], replicated, may hold values from -1 to 1
- value_weight: bfloat16 [256, 2048], replicated, may hold values from -0.375 to 0.375
- up_weight: bfloat16 [2048, 4096], P(None, 'fsdp'), may hold values from -0.125 to 0.125
- down_weight: bfloat16 [4096, 2048], P('fsdp'), may hold values from -0.09375 to 0.09375
- cotangent: bfloat16 [4096, 2048], P(('patch', 'fsdp')), may hold values from -6 to 6
Outputs:
- layer_output: bfloat16 [4096, 2048], P(('patch', 'fsdp'))
- input_grad: bfloat16 [4096, 2048], P(('patch', 'fsdp'))
- up_grad: float32 [2048, 4096], P('patch', 'fsdp')
- down_grad: float32 [4096, 2048], P('fsdp', 'patch')
Inputs may be any that keep to these rules, and one draw needn't show every extreme that they name: `route`: within the rows of one device (aligned blocks of 512 rows) no patch is named by more than 128 rows, and in every block some patch is named by exactly 128.
All inputs are finite; a program needn't handle non-finite values.
Results may differ from a plain program's by a relative error of at most 0.013.
Values may be sent and summed in bfloat16 or wider, within the bound.
A program may use at most 192 MiB of HBM per device.

v0:
```python
import jax
import jax.numpy as jnp
from jax import lax
from jax.experimental import pallas as pl
from jax.experimental.layout import Layout, with_layout_constraint
from jax.experimental.pallas import tpu as pltpu
from jax.sharding import PartitionSpec as P

D = 2048
HEADS = 16
EMPTY = 8.0


eps = 1e-05


def gelu_tanh(values):
    return jax.nn.gelu(values, approximate=True)


def pack_rows(observed, route, patches, capacity):
    targets = route[:, 0]
    onehot = (targets[:, None] == jnp.arange(patches, dtype=jnp.int32)[None, :]).astype(jnp.int32)
    ranks = jnp.sum(onehot * (jnp.cumsum(onehot, axis=0) - 1), axis=1)
    slots = targets * capacity + ranks
    packed = (
        jnp.full((patches * capacity, observed.shape[1]), EMPTY, observed.dtype)
        .at[slots]
        .set(observed)
    )
    return packed.reshape(patches, capacity, observed.shape[1])


def attention_kernel(q_ref, obs_ref, wk_ref, wv_ref, grid_ref, out_ref, rows_ref, k_ref, v_ref, s_ref):
    keys, width = k_ref.shape
    block = min(1024, keys)
    rows = s_ref.shape[0]
    scale = 1.4426950408889634 / width**0.5

    @pl.when(pl.program_id(0) == 0)
    def _():
        for start in range(0, keys, block):
            piece = obs_ref[start : start + block, :]
            live = piece < 0.5 * (EMPTY + 6.0)
            rows_ref[start : start + block, :] = jnp.where(live, piece, jnp.zeros_like(piece))
            v_ref[start : start + block, width:] = jnp.where(
                live[:, :width], jnp.ones_like(piece[:, :width]), jnp.zeros_like(piece[:, :width])
            )

    for start in range(0, keys, block):
        piece = rows_ref[start : start + block, :]
        k_ref[start : start + block, :] = jnp.dot(
            piece, wk_ref[...], preferred_element_type=jnp.float32
        ).astype(jnp.bfloat16)
        v_ref[start : start + block, :width] = jnp.dot(
            piece, wv_ref[...], preferred_element_type=jnp.float32
        ).astype(jnp.bfloat16)

    @pl.loop(0, q_ref.shape[0] // rows)
    def _(index):
        here = pl.ds(pl.multiple_of(index * rows, rows), rows)
        queries = q_ref[here, :]
        peak = jnp.zeros((rows, 128), jnp.float32)
        for start in range(0, keys, block):
            scores = lax.dot_general(
                queries,
                k_ref[start : start + block, :],
                (((1,), (1,)), ((), ())),
                preferred_element_type=jnp.float32,
            )
            s_ref[:, start : start + block] = scores
            for lane in range(0, block, 128):
                peak = jnp.maximum(peak, scores[:, lane : lane + 128])
        rowmax = jnp.max(peak, axis=-1, keepdims=True)
        total = jnp.zeros((rows, 2 * width), jnp.float32)
        for start in range(0, keys, block):
            lifted = jnp.exp2((s_ref[:, start : start + block] - rowmax) * scale)
            total = total + jnp.dot(
                lifted.astype(jnp.bfloat16),
                v_ref[start : start + block, :],
                preferred_element_type=jnp.float32,
            )
        denominator = total[:, width:] + jnp.exp2(-rowmax * scale)
        attended = total[:, :width] / denominator
        out_ref[here, :] = (grid_ref[here, :].astype(jnp.float32) + attended).astype(jnp.bfloat16)


def attend(queries, obs_rows, key_cols, value_cols, grid_cols, head_width):
    tokens, columns = queries.shape
    keys, channels = obs_rows.shape
    rows = min(256, tokens)
    by_head = lambda length: pl.BlockSpec((length, head_width), lambda h: (0, h))
    whole = lambda shape: pl.BlockSpec(shape, lambda h: (0, 0))
    return pl.pallas_call(
        attention_kernel,
        grid=(columns // head_width,),
        in_specs=[
            by_head(tokens),
            whole((keys, channels)),
            by_head(channels),
            by_head(channels),
            by_head(tokens),
        ],
        out_specs=by_head(tokens),
        out_shape=jax.ShapeDtypeStruct((tokens, columns), jnp.bfloat16),
        scratch_shapes=[
            pltpu.VMEM((keys, channels), jnp.bfloat16),
            pltpu.VMEM((keys, head_width), jnp.bfloat16),
            pltpu.VMEM((keys, 2 * head_width), jnp.bfloat16),
            pltpu.VMEM((rows, keys), jnp.float32),
        ],
        compiler_params=pltpu.CompilerParams(vmem_limit_bytes=48 * 1024 * 1024),
        cost_estimate=pl.CostEstimate(
            flops=4 * tokens * keys * columns * 2, bytes_accessed=keys * channels * 4, transcendentals=tokens * keys * 4
        ),
    )(queries, obs_rows, key_cols, value_cols, grid_cols)


def pick(parts, index):
    return lax.dynamic_index_in_dim(parts, index, 0, keepdims=False)


def add(first, second):
    return (first.astype(jnp.float32) + second.astype(jnp.float32)).astype(jnp.bfloat16)


def line_scatter(parts, place, length):
    right = left = None
    for step in range(length - 1):
        send = pick(parts, jnp.clip(length - 1 - step + place, 0, length - 1))
        right = lax.ppermute(
            send if right is None else add(send, right),
            "patch",
            [(2 * a + y, 2 * a + 2 + y) for a in range(step + 1) for y in range(2)],
        )
        send = pick(parts, jnp.clip(step - (length - 1) + place, 0, length - 1))
        left = lax.ppermute(
            send if left is None else add(send, left),
            "patch",
            [(2 * a + y, 2 * a - 2 + y) for a in range(length - 1 - step, length) for y in range(2)],
        )
    total = pick(parts, place).astype(jnp.float32)
    return total if right is None else total + right.astype(jnp.float32) + left.astype(jnp.float32)


def swap_pairs(patches):
    return [(p, p ^ 1) for p in range(patches)]


def scatter_pair_first(partial, patches):
    length = patches // 2
    patch = lax.axis_index("patch")
    place, side = patch // 2, patch % 2
    blocks = partial.reshape(length, 2, -1, partial.shape[1])
    mine = lax.dynamic_index_in_dim(blocks, side, 1, keepdims=False)
    theirs = lax.dynamic_index_in_dim(blocks, 1 - side, 1, keepdims=False)
    return line_scatter(add(mine, lax.ppermute(theirs, "patch", swap_pairs(patches))), place, length)


def scatter_line_first(partial, patches):
    length = patches // 2
    patch = lax.axis_index("patch")
    place, side = patch // 2, patch % 2
    blocks = partial.reshape(length, 2, -1, partial.shape[1])
    pair = line_scatter(blocks, place, length)
    got = lax.ppermute(pick(pair, 1 - side).astype(jnp.bfloat16), "patch", swap_pairs(patches))
    return pick(pair, side) + got.astype(jnp.float32)


def on_device(
    observed,
    route,
    grid,
    gain,
    query_weight,
    key_weight,
    value_weight,
    up_weight,
    down_weight,
    cotangent,
):
    patches = lax.axis_size("patch")
    groups = lax.axis_size("fsdp")
    place = lax.axis_index("fsdp")
    token_count = grid.shape[0]
    head_width = D // HEADS
    columns = query_weight.shape[1]
    capacity = 2 * observed.shape[0] // patches
    all_grid = lax.all_gather(grid, "fsdp", axis=0, tiled=True)
    packed = pack_rows(observed, route, patches, capacity)
    packed = lax.all_to_all(packed, "patch", split_axis=0, concat_axis=0, tiled=True)
    obs_rows = packed.reshape(patches * capacity, observed.shape[1])
    obs_all = lax.all_gather(obs_rows, "fsdp", axis=0, tiled=True)
    queries = jnp.dot(all_grid, query_weight, preferred_element_type=jnp.float32).astype(jnp.bfloat16)
    own_columns = lambda array: lax.dynamic_slice_in_dim(array, place * columns, columns, 1)
    assimilated_columns = attend(
        queries,
        obs_all,
        own_columns(key_weight),
        own_columns(value_weight),
        own_columns(all_grid),
        head_width,
    )
    assimilated = lax.all_gather(assimilated_columns, "fsdp", axis=1, tiled=True)
    all_values = assimilated.astype(jnp.float32)
    all_removed = all_values - jnp.mean(all_values, axis=-1, keepdims=True)
    all_inverse = lax.rsqrt(jnp.mean(all_removed * all_removed, axis=-1, keepdims=True) + eps)
    all_normed = (all_removed * all_inverse * gain).astype(jnp.bfloat16)
    own_rows = lambda array: lax.dynamic_slice_in_dim(array, place * token_count, token_count, 0)
    values32 = own_rows(assimilated).astype(jnp.float32)
    inverse_stddev = own_rows(all_inverse)
    standardized_input = (values32 - jnp.mean(values32, axis=-1, keepdims=True)) * inverse_stddev
    pre = jnp.dot(all_normed, up_weight, preferred_element_type=jnp.float32)
    hidden = gelu_tanh(pre).astype(jnp.bfloat16)
    all_cot = lax.all_gather(cotangent, "fsdp", axis=0, tiled=True)
    half = hidden.shape[1] // 2
    by_rows = lambda array: with_layout_constraint(array, Layout(major_to_minor=(0, 1)))
    part = lambda rows, cols: by_rows(
        lax.dot_general(
            rows, cols, (((0,), (0,)), ((), ())), preferred_element_type=jnp.float32
        ).astype(jnp.bfloat16)
    )
    down_low = scatter_line_first(part(all_cot, hidden[:, :half]), patches)
    down_high = scatter_pair_first(part(all_cot, hidden[:, half:]), patches)
    branch = lax.psum_scatter(
        jnp.dot(hidden, down_weight, preferred_element_type=jnp.float32).astype(jnp.bfloat16),
        "fsdp",
        scatter_dimension=0,
        tiled=True,
    ).astype(jnp.float32)
    layer_output = (values32 + branch).astype(jnp.bfloat16)
    back_hidden = lax.dot_general(
        all_cot, down_weight, (((1,), (1,)), ((), ())), preferred_element_type=jnp.float32
    )
    slope = jax.vjp(gelu_tanh, pre)[1](back_hidden)[0]
    pre_grad = slope.astype(jnp.bfloat16)
    up_low = scatter_pair_first(part(all_normed, pre_grad[:, :half]), patches)
    up_high = scatter_pair_first(part(all_normed, pre_grad[:, half:]), patches)
    normed_grad = lax.psum_scatter(
        lax.dot_general(
            pre_grad, up_weight, (((1,), (1,)), ((), ())), preferred_element_type=jnp.float32
        ).astype(jnp.bfloat16),
        "fsdp",
        scatter_dimension=0,
        tiled=True,
    ).astype(jnp.float32)
    gain_scaled = normed_grad * gain
    input_gradient = inverse_stddev * (
        gain_scaled
        - jnp.mean(gain_scaled, axis=-1, keepdims=True)
        - standardized_input * jnp.mean(gain_scaled * standardized_input, axis=-1, keepdims=True)
    )
    input_grad = (cotangent.astype(jnp.float32) + input_gradient).astype(jnp.bfloat16)
    up_grad = jnp.concatenate([up_low, up_high], axis=1)
    down_grad = by_rows(jnp.concatenate([down_low, down_high], axis=1)).T
    return (layer_output, input_grad, up_grad, down_grad)


def solution(mesh):
    in_specs = (
        P(("patch", "fsdp"), None),
        P(("patch", "fsdp"), None),
        P(("patch", "fsdp"), None),
        P(),
        P(None, "fsdp"),
        P(),
        P(),
        P(None, "fsdp"),
        P("fsdp", None),
        P(("patch", "fsdp"), None),
    )
    out_specs = (
        P(("patch", "fsdp"), None),
        P(("patch", "fsdp"), None),
        P("patch", "fsdp"),
        P("fsdp", "patch"),
    )
    return jax.shard_map(
        on_device, mesh=mesh, in_specs=in_specs, out_specs=out_specs, check_vma=False
    )
```

profile of v0, /device:TPU:0, one launch (start us, length us, event | category | flops | bytes accessed | tf_op | source)
XLA Modules:
  0.0 302.2 jit_solution(4275668228740462776)
XLA Ops:
  8.7 1.1 reduce-window.6
  11.5 2.9 scatter_custom_fusion
  14.4 21.7 %all_to_all.5 = bf16[8,128,256]{2,1,0:T(8,128)(2,1)} all-to-all(bf16[8,128,256]{2,1,0:T(8,128)(2,1)S(1)} %bitcast.146), channel_id=1, replica_groups=mesh['patch'=8,'fsdp'=4] {'patch'}, dimensions={0} | all-to-all | bytes 1048576 | tf_op jit(solution)/shard_map/all_to_all | solution.py:191
  36.9 1.1 constant_dynamic-slice_fusion.1
  38.0 1.1 constant_dynamic-slice_fusion.grid_ref
  39.1 3.6 %convolution_convert_fusion.6.q_ref = bf16[512,512]{1,0:T(8,128)(2,1)} fusion(bf16[512,2048]{1,0:T(8,128)(2,1)} %all-gather.5.cloned.1.call-done, bf16[2048,512]{1,0:T(8,128)(2,1)S(1)} %copy-done), kind=kOutput, calls=%fused_computation.33 | convolution fusion | flops 1074003968 | bytes 4718592 | tf_op jit(solution)/shard_map/dot_general | solution.py:194
  42.8 16.3 %all-gather.7.cloned.1.call-done.obs_ref = bf16[4096,256]{1,0:T(8,128)(2,1)} async-done(((bf16[1024,256]{1,0:T(8,128)(2,1)}), bf16[4096,256]{1,0:T(8,128)(2,1)}) %all-gather.7.cloned.1.call-update) | async-done | bytes 2097168 | tf_op jit(solution)/shard_map/all_gather | solution.py:193
  59.1 1.6 copy-done.2
  60.7 1.0 copy-done.3
  61.7 26.5 %shard_map.129 = bf16[512,512]{1,0:T(8,128)(2,1)} custom-call(bf16[512,512]{1,0:T(8,128)(2,1)S(1)} %copy-done.3, bf16[4096,256]{1,0:T(8,128)(2,1)S(1)} %copy-done.2, bf16[256,512]{1,0:T(8,128)(2,1)S(1)} %get-tuple-element.35.wk_ref, bf16[256,512]{1,0:T(8,128)(2,1)S(1)} %get-tuple-element.34.wv_ref, bf16[512,512]{1,0:T(8,128)(2,1)S(1)} %constant_dynamic-slice_fusion.grid_ref), custom_call_target="tpu_custom_call" | custom-call | flops 8589934592 | bytes 4194304 | tf_op jit(solution)/shard_map/pallas_call | solution.py:94
  88.5 6.5 %fusion.58 = f32[512,1024]{1,0:T(8,128)} fusion(bf16[512,2048]{1,0:T(8,128)(2,1)} %all-gather.11.cloned.1.call-done, bf16[1024,2048]{1,0:T(8,128)(2,1)} %param.18), kind=kOutput, calls=%fused_computation.123 | convolution fusion | flops 2147483648 | bytes 8388608 | tf_op jit(solution)/shard_map/dot_general | solution.py:232
  95.0 16.0 %all-gather.9.cloned.1.call-done = bf16[512,2048]{1,0:T(8,128)(2,1)} async-done(((bf16[512,512]{1,0:T(8,128)(2,1)}), bf16[512,2048]{1,0:T(8,128)(2,1)}) %all-gather.9.cloned.1.call-update) | async-done | bytes 2097168 | tf_op jit(solution)/shard_map/all_gather | solution.py:204
  111.0 2.1 convert_reduce_fusion
  113.9 7.2 %fusion.11 = (bf16[512,1024]{1,0:T(8,128)(2,1)S(1)}, bf16[512,1024]{1,0:T(8,128)(2,1)}) fusion(f32[512,1024]{1,0:T(8,128)S(1)} %copy-done.17, bf16[2048,1024]{1,0:T(8,128)(2,1)} %param.17, bf16[512,2048]{1,0:T(8,128)(2,1)S(1)} %copy-done.4, f32[2048]{0:T(1024)S(1)} %copy-done.12, f32[512]{0:T(512)S(1)} %add_rsqrt_fusion, f32[512]{0:T(512)S(1)} %broadcast_multiply_fusion), kind=kOutput, calls=%fused_computation.22 | convolution fusion | flops 2164260864 | bytes 10498048 | tf_op jit(solution)/shard_map/dot_general | solution.py:213
  121.1 1.0 copy-done.18
  122.1 3.7 %convolution_convert_fusion = bf16[512,2048]{1,0:T(8,128)(2,1)} fusion(bf16[512,1024]{1,0:T(8,128)(2,1)S(1)} %get-tuple-element.20, bf16[2048,1024]{1,0:T(8,128)(2,1)S(1)} %copy-done.13), kind=kOutput, calls=%fused_computation.10 | convolution fusion | flops 2148532224 | bytes 7340032 | tf_op jit(solution)/shard_map/dot_general | solution.py:240
  125.9 3.1 %convolution_convert_fusion.3 = bf16[512,2048]{0,1:T(8,128)(2,1)S(1)} fusion(bf16[512,2048]{1,0:T(8,128)(2,1)} %all-gather.11.cloned.1.call-done, bf16[512,1024]{1,0:T(8,128)(2,1)} %get-tuple-element.21), kind=kOutput, calls=%fused_computation.13 | convolution fusion | flops 1074790400 | bytes 4718592 | tf_op jit(solution)/shard_map/dot_general | solution.py:219
  129.1 1.0 dynamic-slice_bitcast_fusion.4
  130.1 4.5 %collective-permute-start.14 = (bf16[2,256,512]{2,1,0:T(8,128)(2,1)}, bf16[2,256,512]{2,1,0:T(8,128)(2,1)}, u32[]{:S(2)}, u32[]{:S(2)}) collective-permute-start(bf16[2,256,512]{2,1,0:T(8,128)(2,1)} %get-tuple-element.16), channel_id=1, source_target_pairs={{0,8},{4,12},{1,9},{5,13},{2,10},{6,14},{3,11},{7,15}} | collective-permute-start | bytes 1572872 | tf_op jit(solution)/shard_map/ppermute | solution.py:131
  134.6 1.5 collective-permute-start.17
  136.1 1.3 convolution_convert_fusion.2
  137.4 1.0 dynamic-slice_bitcast_fusion
  138.5 1.5 collective-permute-start.21
  140.0 3.0 convolution_convert_fusion.5
  143.0 3.8 %convolution_convert_fusion.1 = bf16[512,2048]{1,0:T(8,128)(2,1)} fusion(bf16[512,1024]{1,0:T(8,128)(2,1)S(1)} %copy-done.16, bf16[1024,2048]{1,0:T(8,128)(2,1)S(1)} %copy-done.14), kind=kOutput, calls=%fused_computation.11 | convolution fusion | flops 2148532224 | bytes 7340032 | tf_op jit(solution)/shard_map/dot_general | solution.py:226
  146.8 2.3 dynamic-slice_bitcast_fusion.2
  149.0 1.0 collective-permute-start
  150.0 2.6 convolution_convert_fusion.4
  152.6 1.3 copy-done.7
  154.0 1.1 collective-permute-start.7
  155.4 1.5 fusion.26
  156.9 1.5 collective-permute-start.15
  158.4 6.5 %collective-permute-done.21 = bf16[4,256,512]{2,1,0:T(8,128)(2,1)} collective-permute-done((bf16[4,256,512]{2,1,0:T(8,128)(2,1)}, bf16[4,256,512]{2,1,0:T(8,128)(2,1)}, u32[]{:S(2)}, u32[]{:S(2)}) %collective-permute-start.21) | collective-permute-done | bytes 1048608 | tf_op jit(solution)/shard_map/ppermute | solution.py:157
  164.8 1.6 fusion.12
  166.5 1.3 collective-permute-start.22
  167.8 19.5 %collective-permute-done = bf16[4,256,512]{2,1,0:T(8,128)(2,1)} collective-permute-done((bf16[4,256,512]{2,1,0:T(8,128)(2,1)}, bf16[4,256,512]{2,1,0:T(8,128)(2,1)}, u32[]{:S(2)}, u32[]{:S(2)}) %collective-permute-start) | collective-permute-done | bytes 1048608 | tf_op jit(solution)/shard_map/ppermute | solution.py:157
  188.1 1.6 fusion.14
  189.7 19.0 %collective-permute-done.7 = bf16[4,256,512]{2,1,0:T(8,128)(2,1)} collective-permute-done((bf16[4,256,512]{2,1,0:T(8,128)(2,1)S(1)}, bf16[4,256,512]{2,1,0:T(8,128)(2,1)}, u32[]{:S(2)}, u32[]{:S(2)}) %collective-permute-start.7) | collective-permute-done | bytes 1048608 | tf_op jit(solution)/shard_map/ppermute | solution.py:157
  208.8 1.4 collective-permute-start.1
  210.2 1.5 fusion.13
  212.5 1.3 collective-permute-start.8
  213.8 1.4 fusion.27
  216.0 1.0 collective-permute-done.1
  216.9 4.4 %collective-permute-start.23 = (bf16[256,512]{1,0:T(8,128)(2,1)S(1)}, bf16[256,512]{1,0:T(8,128)(2,1)S(1)}, u32[]{:S(2)}, u32[]{:S(2)}) collective-permute-start(bf16[256,512]{1,0:T(8,128)(2,1)S(1)} %fusion.36), channel_id=1, source_target_pairs={{0,8},{4,12},{8,16},{12,20},{1,9},{5,13},{9,17},{13,21},{2,10},{6,... | collective-permute-start | bytes 786440 | tf_op jit(solution)/shard_map/ppermute | solution.py:131
  221.4 1.1 collective-permute-done.8
  222.5 4.4 %collective-permute-start.2 = (bf16[256,512]{1,0:T(8,128)(2,1)S(1)}, bf16[256,512]{1,0:T(8,128)(2,1)S(1)}, u32[]{:S(2)}, u32[]{:S(2)}) collective-permute-start(bf16[256,512]{1,0:T(8,128)(2,1)S(1)} %fusion.46), channel_id=1, source_target_pairs={{0,8},{4,12},{8,16},{12,20},{1,9},{5,13},{9,17},{13,21},{2,10},{6,... | collective-permute-start | bytes 786440 | tf_op jit(solution)/shard_map/ppermute | solution.py:131
  228.2 4.4 %collective-permute-start.9 = (bf16[256,512]{1,0:T(8,128)(2,1)S(1)}, bf16[256,512]{1,0:T(8,128)(2,1)S(1)}, u32[]{:S(2)}, u32[]{:S(2)}) collective-permute-start(bf16[256,512]{1,0:T(8,128)(2,1)S(1)} %fusion.41), channel_id=1, source_target_pairs={{0,8},{4,12},{8,16},{12,20},{1,9},{5,13},{9,17},{13,21},{2,10},{6,... | collective-permute-start | bytes 786440 | tf_op jit(solution)/shard_map/ppermute | solution.py:131
  232.7 2.3 collective-permute-start.16
  236.6 2.8 collective-permute-done.9
  239.4 4.4 %collective-permute-start.3 = (bf16[256,512]{1,0:T(8,128)(2,1)S(1)}, bf16[256,512]{1,0:T(8,128)(2,1)S(1)}, u32[]{:S(2)}, u32[]{:S(2)}) collective-permute-start(bf16[256,512]{1,0:T(8,128)(2,1)S(1)} %get-tuple-element.26), channel_id=1, source_target_pairs={{0,8},{4,12},{8,16},{12,20},{16,24},{20,28},{1,9},{5,13},{9,17},{1... | collective-permute-start | bytes 786440 | tf_op jit(solution)/shard_map/ppermute | solution.py:131
  244.8 10.1 %collective-permute-start.10 = (bf16[256,512]{1,0:T(8,128)(2,1)S(1)}, bf16[256,512]{1,0:T(8,128)(2,1)S(1)}, u32[]{:S(2)}, u32[]{:S(2)}) collective-permute-start(bf16[256,512]{1,0:T(8,128)(2,1)S(1)} %get-tuple-element.30), channel_id=1, source_target_pairs={{0,8},{4,12},{8,16},{12,20},{16,24},{20,28},{1,9},{5,13},{9,17},{1... | collective-permute-start | bytes 786440 | tf_op jit(solution)/shard_map/ppermute | solution.py:131
  255.0 1.3 collective-permute-start.6
  256.4 1.3 collective-permute-start.19
  257.7 1.3 collective-permute-start.13
  259.1 7.0 %collective-permute-done.6 = bf16[256,512]{1,0:T(8,128)(2,1)S(1)} collective-permute-done((bf16[256,512]{1,0:T(8,128)(2,1)S(1)}, bf16[256,512]{1,0:T(8,128)(2,1)S(1)}, u32[]{:S(2)}, u32[]{:S(2)}) %collective-permute-start.6) | collective-permute-done | bytes 262176 | tf_op jit(solution)/shard_map/ppermute | solution.py:137
  266.2 3.3 %collective-permute-start.24 = (bf16[256,512]{1,0:T(8,128)(2,1)S(1)}, bf16[256,512]{1,0:T(8,128)(2,1)S(1)}, u32[]{:S(2)}, u32[]{:S(2)}) collective-permute-start(bf16[256,512]{1,0:T(8,128)(2,1)S(1)} %get-tuple-element.22), channel_id=1, source_target_pairs={{0,8},{4,12},{8,16},{12,20},{16,24},{20,28},{1,9},{5,13},{9,17},{1... | collective-permute-start | bytes 786440 | tf_op jit(solution)/shard_map/ppermute | solution.py:131
  269.6 1.3 collective-permute-start.27
  270.9 11.5 %collective-permute-done.13 = bf16[256,512]{1,0:T(8,128)(2,1)S(1)} collective-permute-done((bf16[256,512]{1,0:T(8,128)(2,1)S(1)}, bf16[256,512]{1,0:T(8,128)(2,1)S(1)}, u32[]{:S(2)}, u32[]{:S(2)}) %collective-permute-start.13) | collective-permute-done | bytes 262176 | tf_op jit(solution)/shard_map/ppermute | solution.py:137
  282.8 1.5 collective-permute-start.20
  284.3 1.1 pad_maximum_fusion
  285.4 3.7 %collective-permute-done.20 = bf16[256,512]{1,0:T(8,128)(2,1)S(1)} collective-permute-done((bf16[256,512]{1,0:T(8,128)(2,1)S(1)}, bf16[256,512]{1,0:T(8,128)(2,1)S(1)}, u32[]{:S(2)}, u32[]{:S(2)}) %collective-permute-start.20) | collective-permute-done | bytes 262176 | tf_op jit(solution)/shard_map/ppermute | solution.py:166
  289.4 1.3 copy.20
  290.7 1.6 fusion.29
  292.3 3.1 %fusion.23 = (bf16[128,2048]{1,0:T(8,128)(2,1)}, bf16[128,2048]{1,0:T(8,128)(2,1)}) fusion(bf16[128,2048]{1,0:T(8,128)(2,1)} %reduce-scatter.5.cloned.1.call-done, bf16[128,2048]{1,0:T(8,128)(2,1)} %param.19, f32[128]{0:T(128)S(1)} %broadcast_multiply_fusion.1, f32[128]{0:T(128)S(1)} %broadcast_multiply_fusion.2, f32[128]{0:T(128)S(1)} %broadcast_multiply_fusion.3, ...), kind=kLoop, calls=%fused_computation.42 | loop fusion | flops 3932160 | bytes 3155972 | tf_op jit(solution)/shard_map/convert_element_type | solution.py:253
  (113 shorter events, 12.8 us)
Async XLA Ops:
  7.2 32.0 %copy-start = (bf16[2048,512]{1,0:T(8,128)(2,1)S(1)}, bf16[2048,512]{1,0:T(8,128)(2,1)}, u32[]{:S(2)}) copy-start(bf16[2048,512]{1,0:T(8,128)(2,1)} %param.14) | copy-start | bytes 6291460
  7.2 30.8 %all-gather.5.cloned.1.call-start = ((), (), s32[]{:S(2)}) async-start(), calls=%async_computation.3 | async-start | bytes 2621440 | tf_op jit(solution)/shard_map/all_gather | solution.py:189
  7.9 51.2 %all-gather.7.cloned.1.call-start = ((), (), s32[]{:S(2)}) async-start(), calls=%async_computation.4 | async-start | bytes 2621440 | tf_op jit(solution)/shard_map/all_gather | solution.py:193
  36.1 52.3 %all-gather.11.cloned.1.call-start = ((), (), s32[]{:S(2)}) async-start(), calls=%async_computation.7 | async-start | bytes 2621440 | tf_op jit(solution)/shard_map/all_gather | solution.py:215
  36.9 74.1 %all-gather.9.cloned.1.call-start = ((), (), s32[]{:S(2)}) async-start(), calls=%async_computation.5 | async-start | bytes 2621440 | tf_op jit(solution)/shard_map/all_gather | solution.py:204
  59.1 1.6 copy-start.2
  60.7 1.0 copy-start.3
  88.2 202.5 %reduce-scatter.5.cloned.1.call-start = ((), (), s32[]{:S(2)}) async-start(), calls=%async_computation.8 | async-start | bytes 2621440 | tf_op jit(solution)/shard_map/reduce_scatter | solution.py:239
  111.0 2.2 copy-start.4
  111.0 2.9 copy-start.12
  111.0 2.9 copy-start.17
  113.9 8.2 %copy-start.13 = (bf16[2048,1024]{1,0:T(8,128)(2,1)S(1)}, bf16[2048,1024]{1,0:T(8,128)(2,1)}, u32[]{:S(2)}) copy-start(bf16[2048,1024]{1,0:T(8,128)(2,1)} %param.17) | copy-start | bytes 12582916
  121.1 1.0 copy-start.18
  125.8 166.5 %reduce-scatter.3.cloned.1.call-start = ((), (), s32[]{:S(2)}) async-start(), calls=%async_computation.6 | async-start | bytes 2621440 | tf_op jit(solution)/shard_map/reduce_scatter | solution.py:225
  125.9 10.1 %copy-start.16 = (bf16[512,1024]{1,0:T(8,128)(2,1)S(1)}, bf16[512,1024]{1,0:T(8,128)(2,1)}, u32[]{:S(2)}) copy-start(bf16[512,1024]{1,0:T(8,128)(2,1)} %get-tuple-element.21) | copy-start | bytes 3145732
  129.1 8.3 %copy-start.5 = (bf16[512,2048]{0,1:T(8,128)(2,1)}, bf16[512,2048]{0,1:T(8,128)(2,1)S(1)}, u32[]{:S(2)}) copy-start(bf16[512,2048]{0,1:T(8,128)(2,1)S(1)} %convolution_convert_fusion.3) | copy-start | bytes 6291460
  129.1 7.0 %copy-start.15 = (bf16[512,2048]{1,0:T(8,128)(2,1)S(1)}, bf16[512,2048]{1,0:T(8,128)(2,1)}, u32[]{:S(2)}) copy-start(bf16[512,2048]{1,0:T(8,128)(2,1)} %all-gather.11.cloned.1.call-done) | copy-start | bytes 6291460
  130.1 25.3 %collective-permute-start.14 = (bf16[2,256,512]{2,1,0:T(8,128)(2,1)}, bf16[2,256,512]{2,1,0:T(8,128)(2,1)}, u32[]{:S(2)}, u32[]{:S(2)}) collective-permute-start(bf16[2,256,512]{2,1,0:T(8,128)(2,1)} %get-tuple-element.16), channel_id=1, source_target_pairs={{0,8},{4,12},{1,9},{5,13},{2,10},{6,14},{3,11},{7,15}} | collective-permute-start | bytes 1572872 | tf_op jit(solution)/shard_map/ppermute | solution.py:131
  134.6 77.2 %collective-permute-start.17 = (bf16[2,256,512]{2,1,0:T(8,128)(2,1)}, bf16[2,256,512]{2,1,0:T(8,128)(2,1)}, u32[]{:S(2)}, u32[]{:S(2)}) collective-permute-start(bf16[2,256,512]{2,1,0:T(8,128)(2,1)} %get-tuple-element.17), channel_id=1, source_target_pairs={{24,16},{28,20},{25,17},{29,21},{26,18},{30,22},{27,19},{31,23}} | collective-permute-start | bytes 1572872 | tf_op jit(solution)/shard_map/ppermute | solution.py:137
  137.4 5.6 %copy-start.10 = (bf16[512,2048]{0,1:T(8,128)(2,1)}, bf16[512,2048]{0,1:T(8,128)(2,1)S(1)}, u32[]{:S(2)}) copy-start(bf16[512,2048]{0,1:T(8,128)(2,1)S(1)} %convolution_convert_fusion.2) | copy-start | bytes 6291460
  137.4 2.5 copy-start.19
  138.5 4.5 %copy-start.14 = (bf16[1024,2048]{1,0:T(8,128)(2,1)S(1)}, bf16[1024,2048]{1,0:T(8,128)(2,1)}, u32[]{:S(2)}) copy-start(bf16[1024,2048]{1,0:T(8,128)(2,1)} %param.18) | copy-start | bytes 12582916
  138.5 26.3 %collective-permute-start.21 = (bf16[4,256,512]{2,1,0:T(8,128)(2,1)}, bf16[4,256,512]{2,1,0:T(8,128)(2,1)}, u32[]{:S(2)}, u32[]{:S(2)}) collective-permute-start(bf16[4,256,512]{2,1,0:T(8,128)(2,1)} %dynamic-slice_bitcast_fusion), channel_id=1, source_target_pairs={{0,4},{4,0},{8,12},{12,8},{16,20},{20,16},{24,28},{28,24},{1,5},{5... | collective-permute-start | bytes 3145736 | tf_op jit(solution)/shard_map/ppermute | solution.py:157
  149.0 38.3 %collective-permute-start = (bf16[4,256,512]{2,1,0:T(8,128)(2,1)}, bf16[4,256,512]{2,1,0:T(8,128)(2,1)}, u32[]{:S(2)}, u32[]{:S(2)}) collective-permute-start(bf16[4,256,512]{2,1,0:T(8,128)(2,1)} %dynamic-slice_bitcast_fusion.2), channel_id=1, source_target_pairs={{0,4},{4,0},{8,12},{12,8},{16,20},{20,16},{24,28},{28,24},{1,5},{5... | collective-permute-start | bytes 3145736 | tf_op jit(solution)/shard_map/ppermute | solution.py:157
  152.6 1.3 copy-start.7
  154.0 54.8 %collective-permute-start.7 = (bf16[4,256,512]{2,1,0:T(8,128)(2,1)S(1)}, bf16[4,256,512]{2,1,0:T(8,128)(2,1)}, u32[]{:S(2)}, u32[]{:S(2)}) collective-permute-start(bf16[4,256,512]{2,1,0:T(8,128)(2,1)S(1)} %dynamic-slice_bitcast_fusion.1), channel_id=1, source_target_pairs={{0,4},{4,0},{8,12},{12,8},{16,20},{20,16},{24,28},{28,24},{1,5},{5... | collective-permute-start | bytes 3145736 | tf_op jit(solution)/shard_map/ppermute | solution.py:157
  155.2 9.6 %copy-start.11 = (bf16[512,2048]{0,1:T(8,128)(2,1)S(1)}, bf16[512,2048]{0,1:T(8,128)(2,1)}, u32[]{:S(2)}) copy-start(bf16[512,2048]{0,1:T(8,128)(2,1)} %copy-done.10) | copy-start | bytes 6291460
  156.9 31.2 %copy-start.9 = (bf16[2048,512]{1,0:T(8,128)(2,1)S(1)}, bf16[2048,512]{1,0:T(8,128)(2,1)}, u32[]{:S(2)}) copy-start(bf16[2048,512]{1,0:T(8,128)(2,1)} %convolution_convert_fusion.5) | copy-start | bytes 6291460
  156.9 55.6 %collective-permute-start.15 = (bf16[2,256,512]{2,1,0:T(8,128)(2,1)S(1)}, bf16[2,256,512]{2,1,0:T(8,128)(2,1)S(1)}, u32[]{:S(2)}, u32[]{:S(2)}) collective-permute-start(bf16[2,256,512]{2,1,0:T(8,128)(2,1)S(1)} %fusion.26), channel_id=1, source_target_pairs={{0,8},{4,12},{8,16},{12,20},{1,9},{5,13},{9,17},{13,21},{2,10},{6,... | collective-permute-start | bytes 1572872 | tf_op jit(solution)/shard_map/ppermute | solution.py:131
  166.5 48.7 %collective-permute-start.22 = (bf16[256,512]{1,0:T(8,128)(2,1)S(1)}, bf16[256,512]{1,0:T(8,128)(2,1)S(1)}, u32[]{:S(2)}, u32[]{:S(2)}) collective-permute-start(bf16[256,512]{1,0:T(8,128)(2,1)S(1)} %get-tuple-element.24), channel_id=1, source_target_pairs={{0,8},{4,12},{1,9},{5,13},{2,10},{6,14},{3,11},{7,15}} | collective-permute-start | bytes 786440 | tf_op jit(solution)/shard_map/ppermute | solution.py:131
  187.3 22.9 %copy-start.8 = (bf16[2048,512]{1,0:T(8,128)(2,1)S(1)}, bf16[2048,512]{1,0:T(8,128)(2,1)}, u32[]{:S(2)}) copy-start(bf16[2048,512]{1,0:T(8,128)(2,1)} %copy-done.7) | copy-start | bytes 6291460
  187.3 39.7 %collective-permute-start.25 = (bf16[256,512]{1,0:T(8,128)(2,1)S(1)}, bf16[256,512]{1,0:T(8,128)(2,1)S(1)}, u32[]{:S(2)}, u32[]{:S(2)}) collective-permute-start(bf16[256,512]{1,0:T(8,128)(2,1)S(1)} %get-tuple-element.25), channel_id=1, source_target_pairs={{24,16},{28,20},{25,17},{29,21},{26,18},{30,22},{27,19},{31,23}} | collective-permute-start | bytes 786440 | tf_op jit(solution)/shard_map/ppermute | solution.py:137
  208.8 5.1 %copy-start.6 = (bf16[512,2048]{0,1:T(8,128)(2,1)S(1)}, bf16[512,2048]{0,1:T(8,128)(2,1)}, u32[]{:S(2)}) copy-start(bf16[512,2048]{0,1:T(8,128)(2,1)} %copy-done.5) | copy-start | bytes 6291460
  208.8 8.2 %collective-permute-start.1 = (bf16[256,512]{1,0:T(8,128)(2,1)S(1)}, bf16[256,512]{1,0:T(8,128)(2,1)S(1)}, u32[]{:S(2)}, u32[]{:S(2)}) collective-permute-start(bf16[256,512]{1,0:T(8,128)(2,1)S(1)} %get-tuple-element.28), channel_id=1, source_target_pairs={{0,8},{4,12},{1,9},{5,13},{2,10},{6,14},{3,11},{7,15}} | collective-permute-start | bytes 786440 | tf_op jit(solution)/shard_map/ppermute | solution.py:131
  211.8 20.9 %collective-permute-start.4 = (bf16[256,512]{1,0:T(8,128)(2,1)S(1)}, bf16[256,512]{1,0:T(8,128)(2,1)S(1)}, u32[]{:S(2)}, u32[]{:S(2)}) collective-permute-start(bf16[256,512]{1,0:T(8,128)(2,1)S(1)} %get-tuple-element.29), channel_id=1, source_target_pairs={{24,16},{28,20},{25,17},{29,21},{26,18},{30,22},{27,19},{31,23}} | collective-permute-start | bytes 786440 | tf_op jit(solution)/shard_map/ppermute | solution.py:137
  212.5 10.0 %collective-permute-start.8 = (bf16[256,512]{1,0:T(8,128)(2,1)S(1)}, bf16[256,512]{1,0:T(8,128)(2,1)S(1)}, u32[]{:S(2)}, u32[]{:S(2)}) collective-permute-start(bf16[256,512]{1,0:T(8,128)(2,1)S(1)} %get-tuple-element.32), channel_id=1, source_target_pairs={{0,8},{4,12},{1,9},{5,13},{2,10},{6,14},{3,11},{7,15}} | collective-permute-start | bytes 786440 | tf_op jit(solution)/shard_map/ppermute | solution.py:131
  215.2 20.7 %collective-permute-start.11 = (bf16[256,512]{1,0:T(8,128)(2,1)S(1)}, bf16[256,512]{1,0:T(8,128)(2,1)S(1)}, u32[]{:S(2)}, u32[]{:S(2)}) collective-permute-start(bf16[256,512]{1,0:T(8,128)(2,1)S(1)} %get-tuple-element.33), channel_id=1, source_target_pairs={{24,16},{28,20},{25,17},{29,21},{26,18},{30,22},{27,19},{31,23}} | collective-permute-start | bytes 786440 | tf_op jit(solution)/shard_map/ppermute | solution.py:137
  216.9 11.2 %collective-permute-start.23 = (bf16[256,512]{1,0:T(8,128)(2,1)S(1)}, bf16[256,512]{1,0:T(8,128)(2,1)S(1)}, u32[]{:S(2)}, u32[]{:S(2)}) collective-permute-start(bf16[256,512]{1,0:T(8,128)(2,1)S(1)} %fusion.36), channel_id=1, source_target_pairs={{0,8},{4,12},{8,16},{12,20},{1,9},{5,13},{9,17},{13,21},{2,10},{6,... | collective-permute-start | bytes 786440 | tf_op jit(solution)/shard_map/ppermute | solution.py:131
  222.5 12.5 %collective-permute-start.2 = (bf16[256,512]{1,0:T(8,128)(2,1)S(1)}, bf16[256,512]{1,0:T(8,128)(2,1)S(1)}, u32[]{:S(2)}, u32[]{:S(2)}) collective-permute-start(bf16[256,512]{1,0:T(8,128)(2,1)S(1)} %fusion.46), channel_id=1, source_target_pairs={{0,8},{4,12},{8,16},{12,20},{1,9},{5,13},{9,17},{13,21},{2,10},{6,... | collective-permute-start | bytes 786440 | tf_op jit(solution)/shard_map/ppermute | solution.py:131
  227.0 16.9 %collective-permute-start.18 = (bf16[2,256,512]{2,1,0:T(8,128)(2,1)S(1)}, bf16[2,256,512]{2,1,0:T(8,128)(2,1)S(1)}, u32[]{:S(2)}, u32[]{:S(2)}) collective-permute-start(bf16[2,256,512]{2,1,0:T(8,128)(2,1)S(1)} %get-tuple-element.15), channel_id=1, source_target_pairs={{16,8},{20,12},{24,16},{28,20},{17,9},{21,13},{25,17},{29,21},{18,... | collective-permute-start | bytes 1572872 | tf_op jit(solution)/shard_map/ppermute | solution.py:137
  228.2 11.2 %collective-permute-start.9 = (bf16[256,512]{1,0:T(8,128)(2,1)S(1)}, bf16[256,512]{1,0:T(8,128)(2,1)S(1)}, u32[]{:S(2)}, u32[]{:S(2)}) collective-permute-start(bf16[256,512]{1,0:T(8,128)(2,1)S(1)} %fusion.41), channel_id=1, source_target_pairs={{0,8},{4,12},{8,16},{12,20},{1,9},{5,13},{9,17},{13,21},{2,10},{6,... | collective-permute-start | bytes 786440 | tf_op jit(solution)/shard_map/ppermute | solution.py:131
  232.7 49.8 %collective-permute-start.16 = (bf16[2,256,512]{2,1,0:T(8,128)(2,1)S(1)}, bf16[2,256,512]{2,1,0:T(8,128)(2,1)S(1)}, u32[]{:S(2)}, u32[]{:S(2)}) collective-permute-start(bf16[2,256,512]{2,1,0:T(8,128)(2,1)S(1)} %get-tuple-element.14), channel_id=1, source_target_pairs={{0,8},{4,12},{8,16},{12,20},{16,24},{20,28},{1,9},{5,13},{9,17},{1... | collective-permute-start | bytes 1572872 | tf_op jit(solution)/shard_map/ppermute | solution.py:131
  235.0 21.4 %collective-permute-start.26 = (bf16[256,512]{1,0:T(8,128)(2,1)S(1)}, bf16[256,512]{1,0:T(8,128)(2,1)S(1)}, u32[]{:S(2)}, u32[]{:S(2)}) collective-permute-start(bf16[256,512]{1,0:T(8,128)(2,1)S(1)} %get-tuple-element.23), channel_id=1, source_target_pairs={{16,8},{20,12},{24,16},{28,20},{17,9},{21,13},{25,17},{29,21},{18,... | collective-permute-start | bytes 786440 | tf_op jit(solution)/shard_map/ppermute | solution.py:137
  235.9 8.9 %collective-permute-start.5 = (bf16[256,512]{1,0:T(8,128)(2,1)S(1)}, bf16[256,512]{1,0:T(8,128)(2,1)S(1)}, u32[]{:S(2)}, u32[]{:S(2)}) collective-permute-start(bf16[256,512]{1,0:T(8,128)(2,1)S(1)} %get-tuple-element.27), channel_id=1, source_target_pairs={{16,8},{20,12},{24,16},{28,20},{17,9},{21,13},{25,17},{29,21},{18,... | collective-permute-start | bytes 786440 | tf_op jit(solution)/shard_map/ppermute | solution.py:137
  239.4 18.3 %collective-permute-start.3 = (bf16[256,512]{1,0:T(8,128)(2,1)S(1)}, bf16[256,512]{1,0:T(8,128)(2,1)S(1)}, u32[]{:S(2)}, u32[]{:S(2)}) collective-permute-start(bf16[256,512]{1,0:T(8,128)(2,1)S(1)} %get-tuple-element.26), channel_id=1, source_target_pairs={{0,8},{4,12},{8,16},{12,20},{16,24},{20,28},{1,9},{5,13},{9,17},{1... | collective-permute-start | bytes 786440 | tf_op jit(solution)/shard_map/ppermute | solution.py:131
  244.0 11.1 %collective-permute-start.12 = (bf16[256,512]{1,0:T(8,128)(2,1)S(1)}, bf16[256,512]{1,0:T(8,128)(2,1)S(1)}, u32[]{:S(2)}, u32[]{:S(2)}) collective-permute-start(bf16[256,512]{1,0:T(8,128)(2,1)S(1)} %get-tuple-element.31), channel_id=1, source_target_pairs={{16,8},{20,12},{24,16},{28,20},{17,9},{21,13},{25,17},{29,21},{18,... | collective-permute-start | bytes 786440 | tf_op jit(solution)/shard_map/ppermute | solution.py:137
  244.8 24.8 %collective-permute-start.10 = (bf16[256,512]{1,0:T(8,128)(2,1)S(1)}, bf16[256,512]{1,0:T(8,128)(2,1)S(1)}, u32[]{:S(2)}, u32[]{:S(2)}) collective-permute-start(bf16[256,512]{1,0:T(8,128)(2,1)S(1)} %get-tuple-element.30), channel_id=1, source_target_pairs={{0,8},{4,12},{8,16},{12,20},{16,24},{20,28},{1,9},{5,13},{9,17},{1... | collective-permute-start | bytes 786440 | tf_op jit(solution)/shard_map/ppermute | solution.py:131
  255.0 11.1 %collective-permute-start.6 = (bf16[256,512]{1,0:T(8,128)(2,1)S(1)}, bf16[256,512]{1,0:T(8,128)(2,1)S(1)}, u32[]{:S(2)}, u32[]{:S(2)}) collective-permute-start(bf16[256,512]{1,0:T(8,128)(2,1)S(1)} %fusion.45), channel_id=1, source_target_pairs={{8,0},{12,4},{16,8},{20,12},{24,16},{28,20},{9,1},{13,5},{17,9},{2... | collective-permute-start | bytes 786440 | tf_op jit(solution)/shard_map/ppermute | solution.py:137
  256.4 26.1 %collective-permute-start.19 = (bf16[2,256,512]{2,1,0:T(8,128)(2,1)S(1)}, bf16[2,256,512]{2,1,0:T(8,128)(2,1)S(1)}, u32[]{:S(2)}, u32[]{:S(2)}) collective-permute-start(bf16[2,256,512]{2,1,0:T(8,128)(2,1)S(1)} %fusion.25), channel_id=1, source_target_pairs={{8,0},{12,4},{16,8},{20,12},{24,16},{28,20},{9,1},{13,5},{17,9},{2... | collective-permute-start | bytes 1572872 | tf_op jit(solution)/shard_map/ppermute | solution.py:137
  257.7 24.7 %collective-permute-start.13 = (bf16[256,512]{1,0:T(8,128)(2,1)S(1)}, bf16[256,512]{1,0:T(8,128)(2,1)S(1)}, u32[]{:S(2)}, u32[]{:S(2)}) collective-permute-start(bf16[256,512]{1,0:T(8,128)(2,1)S(1)} %fusion.40), channel_id=1, source_target_pairs={{8,0},{12,4},{16,8},{20,12},{24,16},{28,20},{9,1},{13,5},{17,9},{2... | collective-permute-start | bytes 786440 | tf_op jit(solution)/shard_map/ppermute | solution.py:137
  266.2 19.2 %collective-permute-start.24 = (bf16[256,512]{1,0:T(8,128)(2,1)S(1)}, bf16[256,512]{1,0:T(8,128)(2,1)S(1)}, u32[]{:S(2)}, u32[]{:S(2)}) collective-permute-start(bf16[256,512]{1,0:T(8,128)(2,1)S(1)} %get-tuple-element.22), channel_id=1, source_target_pairs={{0,8},{4,12},{8,16},{12,20},{16,24},{20,28},{1,9},{5,13},{9,17},{1... | collective-permute-start | bytes 786440 | tf_op jit(solution)/shard_map/ppermute | solution.py:131
  269.6 15.7 %collective-permute-start.27 = (bf16[256,512]{1,0:T(8,128)(2,1)S(1)}, bf16[256,512]{1,0:T(8,128)(2,1)S(1)}, u32[]{:S(2)}, u32[]{:S(2)}) collective-permute-start(bf16[256,512]{1,0:T(8,128)(2,1)S(1)} %fusion.35), channel_id=1, source_target_pairs={{8,0},{12,4},{16,8},{20,12},{24,16},{28,20},{9,1},{13,5},{17,9},{2... | collective-permute-start | bytes 786440 | tf_op jit(solution)/shard_map/ppermute | solution.py:137
  282.8 6.4 %collective-permute-start.20 = (bf16[256,512]{1,0:T(8,128)(2,1)S(1)}, bf16[256,512]{1,0:T(8,128)(2,1)S(1)}, u32[]{:S(2)}, u32[]{:S(2)}) collective-permute-start(bf16[256,512]{1,0:T(8,128)(2,1)S(1)} %fusion.49), channel_id=1, source_target_pairs={{0,4},{4,0},{8,12},{12,8},{16,20},{20,16},{24,28},{28,24},{1,5},{5... | collective-permute-start | bytes 786440 | tf_op jit(solution)/shard_map/ppermute | solution.py:166
  289.4 6.0 %copy-start.1 = (bf16[2048,512]{1,0:T(8,128)(2,1)S(1)}, bf16[2048,512]{1,0:T(8,128)(2,1)}, u32[]{:S(2)}) copy-start(bf16[2048,512]{1,0:T(8,128)(2,1)} %param.14) | copy-start | bytes 6291460
Sparse Core Ops, SparseCore 0:
  9.6 25.2 all-gather.4
  36.4 22.5 all-gather.6
  60.6 22.5 all-gather.10
  88.3 22.5 all-gather.8
  125.9 31.4 reduce-scatter.4
  160.0 31.4 reduce-scatter.2
where the time goes:
time: 303 us; the launch traced here: 302 us
  waiting for transfers between devices  106 us (35%)
  starting transfers between devices  60.3 us (20%)
  matrix products  34.9 us (12%)
  Pallas kernels  26.5 us (9%)
  blocking collectives  21.7 us (7%)
  other arithmetic  21.2 us (7%)
  local copies, waits for them, and re-layouts  16.3 us (5%)
  between operations  14.8 us (5%)
    ppermute x3, waiting for transfers between devices, scatter_pair_first(): lax.ppermute(theirs, 'patch', swap_pairs(patches))  45 us
    ppermute x12, starting transfers between devices, line_scatter(): lax.ppermute(send if right is None else add(send, right), 'patch', [(2 *...  43.2 us
    pallas_call x1, Pallas kernels, attend(): pl.pallas_call(attention_kernel, grid=(columns // head_width,), in_specs=...  26.5 us
    all_to_all x1, blocking collectives, on_device(): lax.all_to_all(packed, 'patch', split_axis=0, concat_axis=0, tiled=True)  21.7 us
    ppermute x12, waiting for transfers between devices, line_scatter(): lax.ppermute(send if left is None else add(send, left), 'patch', [(2 * a...  18.5 us
    all_gather x1, waiting for transfers between devices, on_device(): obs_all = lax.all_gather(obs_rows, 'fsdp', axis=0, tiled=True)  16.3 us
    all_gather x1, waiting for transfers between devices, on_device(): lax.all_gather(assimilated_columns, 'fsdp', axis=1, tiled=True)  16 us
    ppermute x12, starting transfers between devices, line_scatter(): lax.ppermute(send if left is None else add(send, left), 'patch', [(2 * a...  11.5 us
  transfers between devices with their start and end apart: 34, of which 12 were waited for; matrix products, arithmetic and copies ran while one was open for 17% of the time, Pallas kernels for 9%

commit v1 on v0

--- a/solution.py
+++ b/solution.py
@@ -125,22 +125,18 @@
 
 
 def line_scatter(parts, place, length):
-    right = left = None
-    for step in range(length - 1):
-        send = pick(parts, jnp.clip(length - 1 - step + place, 0, length - 1))
-        right = lax.ppermute(
-            send if right is None else add(send, right),
+    total = pick(parts, place).astype(jnp.float32)
+    received = [
+        lax.ppermute(
+            pick(parts, lax.rem(place + shift, length)),
             "patch",
-            [(2 * a + y, 2 * a + 2 + y) for a in range(step + 1) for y in range(2)],
+            [(2 * a + y, 2 * ((a + shift) % length) + y) for a in range(length) for y in range(2)],
         )
-        send = pick(parts, jnp.clip(step - (length - 1) + place, 0, length - 1))
-        left = lax.ppermute(
-            send if left is None else add(send, left),
-            "patch",
-            [(2 * a + y, 2 * a - 2 + y) for a in range(length - 1 - step, length) for y in range(2)],
-        )
-    total = pick(parts, place).astype(jnp.float32)
-    return total if right is None else total + right.astype(jnp.float32) + left.astype(jnp.float32)
+        for shift in range(1, length)
+    ]
+    for block in received:
+        total = total + block.astype(jnp.float32)
+    return total
 
 
 def swap_pairs(patches):

time: 303 us -> 274 us (0.904)
  starting transfers between devices: 60.3 us -> 34.6 us
    ppermute x3, waiting for transfers between devices: 45 us -> 10.9 us  [scatter_pair_first(): lax.ppermute(theirs, 'patch', swap_pairs(patches))]
    ppermute x24 -> x12, waiting for transfers between devices: 23.9 us -> 52.6 us  [line_scatter(): lax.ppermute(pick(parts, lax.rem(place + shift, length)), 'patch', [(2 *...]
    ppermute x24 -> x12, starting transfers between devices: 54.7 us -> 29.6 us  [line_scatter(): lax.ppermute(pick(parts, lax.rem(place + shift, length)), 'patch', [(2 *...]
    convert_element_type x15 -> x3, other arithmetic: 8.55 us -> 3.5 us  [add(): (first.astype(jnp.float32) + second.astype(jnp.float32)).astype(jnp.bfloa...]
    add x4, other arithmetic: 0.49 us -> 4.38 us  [line_scatter(): total = total + block.astype(jnp.float32)]
    ppermute x1, waiting for transfers between devices: 3.74 us -> 7.26 us  [scatter_line_first(): lax.ppermute(pick(pair, 1 - side).astype(jnp.bfloat16), 'patch', swap_pai...]
    unnamed x41 -> x35, local copies, waits for them, and re-layouts: 6.4 us -> 5.84 us
  transfers between devices with their start and end apart: 34 -> 22, of which waited for: 12 -> 10; matrix products, arithmetic and copies ran while one was open for 17% -> 18% of each run, Pallas kernels for 9% -> 10%
where the time goes in v1:
time: 274 us; the launch traced here: 272 us
  waiting for transfers between devices  105 us (38%)
  starting transfers between devices  34.6 us (13%)
  matrix products  33.5 us (12%)
  Pallas kernels  26.5 us (10%)
  blocking collectives  21.7 us (8%)
  other arithmetic  20 us (7%)
  local copies, waits for them, and re-layouts  16.5 us (6%)
  between operations  14.5 us (5%)
    ppermute x12, waiting for transfers between devices, line_scatter(): lax.ppermute(pick(parts, lax.rem(place + shift, length)), 'patch', [(2 *...  52.6 us
    ppermute x12, starting transfers between devices, line_scatter(): lax.ppermute(pick(parts, lax.rem(place + shift, length)), 'patch', [(2 *...  29.6 us
    pallas_call x1, Pallas kernels, attend(): pl.pallas_call(attention_kernel, grid=(columns // head_width,), in_specs=...  26.5 us
    all_to_all x1, blocking collectives, on_device(): lax.all_to_all(packed, 'patch', split_axis=0, concat_axis=0, tiled=True)  21.7 us
    all_gather x1, waiting for transfers between devices, on_device(): obs_all = lax.all_gather(obs_rows, 'fsdp', axis=0, tiled=True)  16.3 us
    all_gather x1, waiting for transfers between devices, on_device(): lax.all_gather(assimilated_columns, 'fsdp', axis=1, tiled=True)  16 us
    ppermute x3, waiting for transfers between devices, scatter_pair_first(): lax.ppermute(theirs, 'patch', swap_pairs(patches))  10.9 us
    dot_general x4, matrix products, on_device(): lax.dot_general(rows, cols, (((0,), (0,)), ((), ())), preferred_element_t...  9.89 us
  transfers between devices with their start and end apart: 22, of which 10 were waited for; matrix products, arithmetic and copies ran while one was open for 18% of the time, Pallas kernels for 10%

profile of v1, /device:TPU:0, one launch (start us, length us, event | category | flops | bytes accessed | tf_op | source)
XLA Modules:
  0.0 271.9 jit_solution(14454627346989016274)
XLA Ops:
  7.2 0.7 all-gather.5.cloned.1.call-update
  8.0 0.7 fusion.41
  8.7 1.1 reduce-window.6
  10.0 0.8 fusion.40
  10.8 0.7 compare_select_fusion
  11.5 2.9 %scatter_custom_fusion = bf16[1024,256]{1,0:T(8,128)(2,1)S(1)} fusion(s32[512]{0:T(512)S(1)} %bitcast.107, bf16[512,256]{1,0:T(8,128)(2,1)} %param.10, bf16[]{:T(256)} %constant.133.clone.1), kind=kCustom, calls=%fused_computation.81 | custom fusion | bytes 524800 | tf_op jit(solution)/shard_map/scatter | solution.py:29
  14.4 21.7 %all_to_all.5 = bf16[8,128,256]{2,1,0:T(8,128)(2,1)} all-to-all(bf16[8,128,256]{2,1,0:T(8,128)(2,1)S(1)} %bitcast.103), channel_id=1, replica_groups=mesh['patch'=8,'fsdp'=4] {'patch'}, dimensions={0} | all-to-all | bytes 1048576 | tf_op jit(solution)/shard_map/all_to_all | solution.py:187
  36.2 0.7 all-gather.11.cloned.1.call-update
  36.9 1.1 constant_dynamic-slice_fusion.1
  38.0 1.1 constant_dynamic-slice_fusion.grid_ref
  39.1 3.6 %convolution_convert_fusion.6.q_ref = bf16[512,512]{1,0:T(8,128)(2,1)} fusion(bf16[512,2048]{1,0:T(8,128)(2,1)} %all-gather.5.cloned.1.call-done, bf16[2048,512]{1,0:T(8,128)(2,1)S(1)} %copy-done), kind=kOutput, calls=%fused_computation.33 | convolution fusion | flops 1074003968 | bytes 4718592 | tf_op jit(solution)/shard_map/dot_general | solution.py:190
  42.8 16.3 %all-gather.7.cloned.1.call-done.obs_ref = bf16[4096,256]{1,0:T(8,128)(2,1)} async-done(((bf16[1024,256]{1,0:T(8,128)(2,1)}), bf16[4096,256]{1,0:T(8,128)(2,1)}) %all-gather.7.cloned.1.call-update) | async-done | bytes 2097168 | tf_op jit(solution)/shard_map/all_gather | solution.py:189
  59.1 1.6 copy-done.2
  60.7 1.0 copy-done.3
  61.7 26.5 %shard_map.129 = bf16[512,512]{1,0:T(8,128)(2,1)} custom-call(bf16[512,512]{1,0:T(8,128)(2,1)S(1)} %copy-done.3, bf16[4096,256]{1,0:T(8,128)(2,1)S(1)} %copy-done.2, bf16[256,512]{1,0:T(8,128)(2,1)S(1)} %get-tuple-element.31.wk_ref, bf16[256,512]{1,0:T(8,128)(2,1)S(1)} %get-tuple-element.30.wv_ref, bf16[512,512]{1,0:T(8,128)(2,1)S(1)} %constant_dynamic-slice_fusion.grid_ref), custom_call_target="tpu_custom_call" | custom-call | flops 8589934592 | bytes 4194304 | tf_op jit(solution)/shard_map/pallas_call | solution.py:94
  88.2 0.2 reduce-scatter.5.cloned.1.call-start
  88.5 6.5 %fusion.46 = f32[512,1024]{1,0:T(8,128)} fusion(bf16[512,2048]{1,0:T(8,128)(2,1)} %all-gather.11.cloned.1.call-done, bf16[1024,2048]{1,0:T(8,128)(2,1)} %param.18), kind=kOutput, calls=%fused_computation.99 | convolution fusion | flops 2147483648 | bytes 8388608 | tf_op jit(solution)/shard_map/dot_general | solution.py:228
  95.0 16.0 %all-gather.9.cloned.1.call-done = bf16[512,2048]{1,0:T(8,128)(2,1)} async-done(((bf16[512,512]{1,0:T(8,128)(2,1)}), bf16[512,2048]{1,0:T(8,128)(2,1)}) %all-gather.9.cloned.1.call-update) | async-done | bytes 2097168 | tf_op jit(solution)/shard_map/all_gather | solution.py:200
  111.0 2.1 convert_reduce_fusion
  113.2 0.7 fusion.2
  113.9 6.0 %fusion.11 = (bf16[512,1024]{1,0:T(8,128)(2,1)S(1)}, bf16[512,1024]{1,0:T(8,128)(2,1)S(1)}) fusion(f32[512,1024]{1,0:T(8,128)S(1)} %copy-done.14, bf16[2048,1024]{1,0:T(8,128)(2,1)} %param.17, bf16[512,2048]{1,0:T(8,128)(2,1)S(1)} %copy-done.4, f32[2048]{0:T(1024)S(1)} %copy-done.10, f32[512]{0:T(512)S(1)} %add_rsqrt_fusion, f32[512]{0:T(512)S(1)} %broadcast_multiply_fusion), kind=kOutput, calls=%fused_computation.22 | convolution fusion | flops 2164260864 | bytes 10498048 | tf_op jit(solution)/shard_map/dot_general | solution.py:209
  120.0 1.0 copy-done.15
  120.9 3.7 %convolution_convert_fusion = bf16[512,2048]{1,0:T(8,128)(2,1)} fusion(bf16[512,1024]{1,0:T(8,128)(2,1)S(1)} %get-tuple-element.19, bf16[2048,1024]{1,0:T(8,128)(2,1)S(1)} %copy-done.11), kind=kOutput, calls=%fused_computation.10 | convolution fusion | flops 2148532224 | bytes 7340032 | tf_op jit(solution)/shard_map/dot_general | solution.py:236
  124.8 2.9 %convolution_convert_fusion.3 = bf16[512,2048]{0,1:T(8,128)(2,1)S(1)} fusion(bf16[512,2048]{1,0:T(8,128)(2,1)} %all-gather.11.cloned.1.call-done, bf16[512,1024]{1,0:T(8,128)(2,1)S(1)} %get-tuple-element.20), kind=kOutput, calls=%fused_computation.13 | convolution fusion | flops 1074790400 | bytes 4718592 | tf_op jit(solution)/shard_map/dot_general | solution.py:215
  127.7 1.2 dynamic-slice_bitcast_fusion.5
  128.9 3.3 %collective-permute-start.10 = (bf16[2,256,512]{2,1,0:T(8,128)(2,1)}, bf16[2,256,512]{2,1,0:T(8,128)(2,1)}, u32[]{:S(2)}, u32[]{:S(2)}) collective-permute-start(bf16[2,256,512]{2,1,0:T(8,128)(2,1)} %get-tuple-element.15), channel_id=1, source_target_pairs={{0,24},{4,28},{8,0},{12,4},{16,8},{20,12},{24,16},{28,20},{1,25},{... | collective-permute-start | bytes 1572872 | tf_op jit(solution)/shard_map/ppermute | solution.py:130
  132.2 1.1 collective-permute-start.9
  133.3 1.3 convolution_convert_fusion.2
  134.7 1.0 dynamic-slice_bitcast_fusion
  135.7 1.5 collective-permute-start.12
  137.2 3.0 %convolution_convert_fusion.5 = bf16[2048,512]{1,0:T(8,128)(2,1)} fusion(bf16[512,1024]{1,0:T(8,128)(2,1)S(1)} %copy-done.16, bf16[512,2048]{1,0:T(8,128)(2,1)S(1)} %copy-done.4, f32[2048]{0:T(1024)S(1)} %copy-done.10, f32[512]{0:T(512)S(1)} %add_rsqrt_fusion, f32[512]{0:T(512)S(1)} %broadcast_multiply_fusion), kind=kOutput, calls=%fused_computation.15 | convolution fusion | flops 1080033280 | bytes 4730880 | tf_op jit(solution)/shard_map/dot_general | solution.py:215
  140.2 3.7 %convolution_convert_fusion.1 = bf16[512,2048]{1,0:T(8,128)(2,1)} fusion(bf16[512,1024]{1,0:T(8,128)(2,1)S(1)} %get-tuple-element.20, bf16[1024,2048]{1,0:T(8,128)(2,1)S(1)} %copy-done.12), kind=kOutput, calls=%fused_computation.11 | convolution fusion | flops 2148532224 | bytes 7340032 | tf_op jit(solution)/shard_map/dot_general | solution.py:222
  143.9 1.3 dynamic-slice_bitcast_fusion.2
  145.2 1.0 collective-permute-start
  146.3 2.7 convolution_convert_fusion.4
  149.0 8.2 %collective-permute-done.8 = bf16[2,256,512]{2,1,0:T(8,128)(2,1)} collective-permute-done((bf16[2,256,512]{2,1,0:T(8,128)(2,1)}, bf16[2,256,512]{2,1,0:T(8,128)(2,1)}, u32[]{:S(2)}, u32[]{:S(2)}) %collective-permute-start.8) | collective-permute-done | bytes 524320 | tf_op jit(solution)/shard_map/ppermute | solution.py:130
  157.1 20.7 %collective-permute-done.9 = bf16[2,256,512]{2,1,0:T(8,128)(2,1)} collective-permute-done((bf16[2,256,512]{2,1,0:T(8,128)(2,1)}, bf16[2,256,512]{2,1,0:T(8,128)(2,1)}, u32[]{:S(2)}, u32[]{:S(2)}) %collective-permute-start.9) | collective-permute-done | bytes 524320 | tf_op jit(solution)/shard_map/ppermute | solution.py:130
  177.9 1.8 fusion.25
  179.7 1.6 collective-permute-start.11
  181.4 0.6 collective-permute-start.4
  182.2 7.3 %collective-permute-done.11 = bf16[256,512]{1,0:T(8,128)(2,1)S(1)} collective-permute-done((bf16[256,512]{1,0:T(8,128)(2,1)S(1)}, bf16[256,512]{1,0:T(8,128)(2,1)S(1)}, u32[]{:S(2)}, u32[]{:S(2)}) %collective-permute-start.11) | collective-permute-done | bytes 262176 | tf_op jit(solution)/shard_map/ppermute | solution.py:162
  189.6 1.7 fusion.12
  191.3 4.0 %collective-permute-start.13 = (bf16[256,512]{1,0:T(8,128)(2,1)S(1)}, bf16[256,512]{1,0:T(8,128)(2,1)S(1)}, u32[]{:S(2)}, u32[]{:S(2)}) collective-permute-start(bf16[256,512]{1,0:T(8,128)(2,1)S(1)} %get-tuple-element.21), channel_id=1, source_target_pairs={{0,8},{4,12},{8,16},{12,20},{16,24},{20,28},{24,0},{28,4},{1,9},{5... | collective-permute-start | bytes 786440 | tf_op jit(solution)/shard_map/ppermute | solution.py:130
  195.3 2.4 collective-permute-start.15
  197.7 1.5 fusion.14
  199.3 0.8 dynamic-slice_bitcast_fusion.14
  200.0 10.9 %collective-permute-done.4 = bf16[4,256,512]{2,1,0:T(8,128)(2,1)S(1)} collective-permute-done((bf16[4,256,512]{2,1,0:T(8,128)(2,1)S(1)}, bf16[4,256,512]{2,1,0:T(8,128)(2,1)S(1)}, u32[]{:S(2)}, u32[]{:S(2)}) %collective-permute-start.4) | collective-permute-done | bytes 1048608 | tf_op jit(solution)/shard_map/ppermute | solution.py:153
  210.9 2.1 collective-permute-start.2
  213.0 0.3 fusion.13
  213.3 0.9 dynamic-slice_bitcast_fusion.11
  214.2 3.5 %collective-permute-start.3 = (bf16[256,512]{1,0:T(8,128)(2,1)S(1)}, bf16[256,512]{1,0:T(8,128)(2,1)}, u32[]{:S(2)}, u32[]{:S(2)}) collective-permute-start(bf16[256,512]{1,0:T(8,128)(2,1)S(1)} %get-tuple-element.25), channel_id=1, source_target_pairs={{0,24},{4,28},{8,0},{12,4},{16,8},{20,12},{24,16},{28,20},{1,25},{... | collective-permute-start | bytes 786440 | tf_op jit(solution)/shard_map/ppermute | solution.py:130
  217.8 2.6 collective-permute-done.14
  220.4 9.2 %collective-permute-start.5 = (bf16[256,512]{1,0:T(8,128)(2,1)}, bf16[256,512]{1,0:T(8,128)(2,1)}, u32[]{:S(2)}, u32[]{:S(2)}) collective-permute-start(bf16[256,512]{1,0:T(8,128)(2,1)} %get-tuple-element.27), channel_id=1, source_target_pairs={{0,8},{4,12},{8,16},{12,20},{16,24},{20,28},{24,0},{28,4},{1,9},{5... | collective-permute-start | bytes 786440 | tf_op jit(solution)/shard_map/ppermute | solution.py:130
  229.6 3.9 %collective-permute-start.6 = (bf16[256,512]{1,0:T(8,128)(2,1)}, bf16[256,512]{1,0:T(8,128)(2,1)}, u32[]{:S(2)}, u32[]{:S(2)}) collective-permute-start(bf16[256,512]{1,0:T(8,128)(2,1)} %get-tuple-element.29), channel_id=1, source_target_pairs={{0,16},{4,20},{8,24},{12,28},{16,0},{20,4},{24,8},{28,12},{1,17},{... | collective-permute-start | bytes 786440 | tf_op jit(solution)/shard_map/ppermute | solution.py:130
  233.6 0.8 copy-done.9
  234.5 1.3 copy.20
  235.8 9.0 %collective-permute-done.2 = bf16[256,512]{1,0:T(8,128)(2,1)} collective-permute-done((bf16[256,512]{1,0:T(8,128)(2,1)}, bf16[256,512]{1,0:T(8,128)(2,1)}, u32[]{:S(2)}, u32[]{:S(2)}) %collective-permute-start.2) | collective-permute-done | bytes 262176 | tf_op jit(solution)/shard_map/ppermute | solution.py:130
  244.8 1.2 fusion.36
  246.0 10.0 %collective-permute-done.6 = bf16[256,512]{1,0:T(8,128)(2,1)} collective-permute-done((bf16[256,512]{1,0:T(8,128)(2,1)}, bf16[256,512]{1,0:T(8,128)(2,1)}, u32[]{:S(2)}, u32[]{:S(2)}) %collective-permute-start.6) | collective-permute-done | bytes 262176 | tf_op jit(solution)/shard_map/ppermute | solution.py:130
  256.1 2.0 collective-permute-done.7
  258.1 1.2 fusion.34
  259.3 1.1 pad_maximum_fusion
  260.4 1.6 fusion.26
  262.0 3.1 %fusion.23 = (bf16[128,2048]{1,0:T(8,128)(2,1)}, bf16[128,2048]{1,0:T(8,128)(2,1)}) fusion(bf16[128,2048]{1,0:T(8,128)(2,1)} %reduce-scatter.5.cloned.1.call-done, bf16[128,2048]{1,0:T(8,128)(2,1)} %param.19, f32[128]{0:T(128)S(1)} %broadcast_multiply_fusion.1, f32[128]{0:T(128)S(1)} %broadcast_multiply_fusion.2, f32[128]{0:T(128)S(1)} %broadcast_multiply_fusion.3, ...), kind=kLoop, calls=%fused_computation.42 | loop fusion | flops 3932160 | bytes 3155972 | tf_op jit(solution)/shard_map/convert_element_type | solution.py:249
  (71 shorter events, 1.5 us)
Async XLA Ops:
  7.2 32.0 %copy-start = (bf16[2048,512]{1,0:T(8,128)(2,1)S(1)}, bf16[2048,512]{1,0:T(8,128)(2,1)}, u32[]{:S(2)}) copy-start(bf16[2048,512]{1,0:T(8,128)(2,1)} %param.14) | copy-start | bytes 6291460
  7.2 30.8 %all-gather.5.cloned.1.call-start = ((), (), s32[]{:S(2)}) async-start(), calls=%async_computation.3 | async-start | bytes 2621440 | tf_op jit(solution)/shard_map/all_gather | solution.py:185
  7.9 51.2 %all-gather.7.cloned.1.call-start = ((), (), s32[]{:S(2)}) async-start(), calls=%async_computation.4 | async-start | bytes 2621440 | tf_op jit(solution)/shard_map/all_gather | solution.py:189
  36.1 52.3 %all-gather.11.cloned.1.call-start = ((), (), s32[]{:S(2)}) async-start(), calls=%async_computation.7 | async-start | bytes 2621440 | tf_op jit(solution)/shard_map/all_gather | solution.py:211
  36.9 74.1 %all-gather.9.cloned.1.call-start = ((), (), s32[]{:S(2)}) async-start(), calls=%async_computation.5 | async-start | bytes 2621440 | tf_op jit(solution)/shard_map/all_gather | solution.py:200
  59.1 1.6 copy-start.2
  60.7 1.0 copy-start.3
  88.2 172.1 %reduce-scatter.5.cloned.1.call-start = ((), (), s32[]{:S(2)}) async-start(), calls=%async_computation.8 | async-start | bytes 2621440 | tf_op jit(solution)/shard_map/reduce_scatter | solution.py:235
  111.0 2.2 copy-start.4
  111.0 2.9 %copy-start.10 = (f32[2048]{0:T(1024)S(1)}, f32[2048]{0:T(1024)}, u32[]{:S(2)}) copy-start(f32[2048]{0:T(1024)} %param.13) | copy-start | bytes 24580
  111.0 2.9 %copy-start.14 = (f32[512,1024]{1,0:T(8,128)S(1)}, f32[512,1024]{1,0:T(8,128)}, u32[]{:S(2)}) copy-start(f32[512,1024]{1,0:T(8,128)} %fusion.46) | copy-start | bytes 6291460
  113.9 7.0 %copy-start.11 = (bf16[2048,1024]{1,0:T(8,128)(2,1)S(1)}, bf16[2048,1024]{1,0:T(8,128)(2,1)}, u32[]{:S(2)}) copy-start(bf16[2048,1024]{1,0:T(8,128)(2,1)} %param.17) | copy-start | bytes 12582916
  120.0 1.0 copy-start.15
  124.7 137.3 %reduce-scatter.3.cloned.1.call-start = ((), (), s32[]{:S(2)}) async-start(), calls=%async_computation.6 | async-start | bytes 2621440 | tf_op jit(solution)/shard_map/reduce_scatter | solution.py:221
  127.7 4.5 %copy-start.8 = (bf16[512,2048]{0,1:T(8,128)(2,1)}, bf16[512,2048]{0,1:T(8,128)(2,1)S(1)}, u32[]{:S(2)}) copy-start(bf16[512,2048]{0,1:T(8,128)(2,1)S(1)} %convolution_convert_fusion.3) | copy-start | bytes 6291460
  127.7 5.6 %copy-start.13 = (bf16[512,2048]{1,0:T(8,128)(2,1)S(1)}, bf16[512,2048]{1,0:T(8,128)(2,1)}, u32[]{:S(2)}) copy-start(bf16[512,2048]{1,0:T(8,128)(2,1)} %all-gather.11.cloned.1.call-done) | copy-start | bytes 6291460
  128.9 20.1 %collective-permute-start.10 = (bf16[2,256,512]{2,1,0:T(8,128)(2,1)}, bf16[2,256,512]{2,1,0:T(8,128)(2,1)}, u32[]{:S(2)}, u32[]{:S(2)}) collective-permute-start(bf16[2,256,512]{2,1,0:T(8,128)(2,1)} %get-tuple-element.15), channel_id=1, source_target_pairs={{0,24},{4,28},{8,0},{12,4},{16,8},{20,12},{24,16},{28,20},{1,25},{... | collective-permute-start | bytes 1572872 | tf_op jit(solution)/shard_map/ppermute | solution.py:130
  132.2 24.9 %collective-permute-start.8 = (bf16[2,256,512]{2,1,0:T(8,128)(2,1)}, bf16[2,256,512]{2,1,0:T(8,128)(2,1)}, u32[]{:S(2)}, u32[]{:S(2)}) collective-permute-start(bf16[2,256,512]{2,1,0:T(8,128)(2,1)} %get-tuple-element.14), channel_id=1, source_target_pairs={{0,8},{4,12},{8,16},{12,20},{16,24},{20,28},{24,0},{28,4},{1,9},{5... | collective-permute-start | bytes 1572872 | tf_op jit(solution)/shard_map/ppermute | solution.py:130
  132.2 45.7 %collective-permute-start.9 = (bf16[2,256,512]{2,1,0:T(8,128)(2,1)}, bf16[2,256,512]{2,1,0:T(8,128)(2,1)}, u32[]{:S(2)}, u32[]{:S(2)}) collective-permute-start(bf16[2,256,512]{2,1,0:T(8,128)(2,1)} %get-tuple-element.16), channel_id=1, source_target_pairs={{0,16},{4,20},{8,24},{12,28},{16,0},{20,4},{24,8},{28,12},{1,17},{... | collective-permute-start | bytes 1572872 | tf_op jit(solution)/shard_map/ppermute | solution.py:130
  134.6 5.6 %copy-start.6 = (bf16[512,2048]{0,1:T(8,128)(2,1)}, bf16[512,2048]{0,1:T(8,128)(2,1)S(1)}, u32[]{:S(2)}) copy-start(bf16[512,2048]{0,1:T(8,128)(2,1)S(1)} %convolution_convert_fusion.2) | copy-start | bytes 6291460
  134.7 2.5 copy-start.16
  135.7 4.5 %copy-start.12 = (bf16[1024,2048]{1,0:T(8,128)(2,1)S(1)}, bf16[1024,2048]{1,0:T(8,128)(2,1)}, u32[]{:S(2)}) copy-start(bf16[1024,2048]{1,0:T(8,128)(2,1)} %param.18) | copy-start | bytes 12582916
  135.7 53.8 %collective-permute-start.12 = (bf16[4,256,512]{2,1,0:T(8,128)(2,1)}, bf16[4,256,512]{2,1,0:T(8,128)(2,1)}, u32[]{:S(2)}, u32[]{:S(2)}) collective-permute-start(bf16[4,256,512]{2,1,0:T(8,128)(2,1)} %dynamic-slice_bitcast_fusion), channel_id=1, source_target_pairs={{0,4},{4,0},{8,12},{12,8},{16,20},{20,16},{24,28},{28,24},{1,5},{5... | collective-permute-start | bytes 3145736 | tf_op jit(solution)/shard_map/ppermute | solution.py:153
  145.2 52.5 %collective-permute-start = (bf16[4,256,512]{2,1,0:T(8,128)(2,1)S(1)}, bf16[4,256,512]{2,1,0:T(8,128)(2,1)}, u32[]{:S(2)}, u32[]{:S(2)}) collective-permute-start(bf16[4,256,512]{2,1,0:T(8,128)(2,1)S(1)} %dynamic-slice_bitcast_fusion.2), channel_id=1, source_target_pairs={{0,4},{4,0},{8,12},{12,8},{16,20},{20,16},{24,28},{28,24},{1,5},{5... | collective-permute-start | bytes 3145736 | tf_op jit(solution)/shard_map/ppermute | solution.py:153
  179.7 9.8 %copy-start.7 = (bf16[512,2048]{0,1:T(8,128)(2,1)S(1)}, bf16[512,2048]{0,1:T(8,128)(2,1)}, u32[]{:S(2)}) copy-start(bf16[512,2048]{0,1:T(8,128)(2,1)} %copy-done.6) | copy-start | bytes 6291460
  179.7 9.7 %collective-permute-start.11 = (bf16[256,512]{1,0:T(8,128)(2,1)S(1)}, bf16[256,512]{1,0:T(8,128)(2,1)S(1)}, u32[]{:S(2)}, u32[]{:S(2)}) collective-permute-start(bf16[256,512]{1,0:T(8,128)(2,1)S(1)} %fusion.37), channel_id=1, source_target_pairs={{0,4},{4,0},{8,12},{12,8},{16,20},{20,16},{24,28},{28,24},{1,5},{5... | collective-permute-start | bytes 786440 | tf_op jit(solution)/shard_map/ppermute | solution.py:162
  181.4 29.6 %collective-permute-start.4 = (bf16[4,256,512]{2,1,0:T(8,128)(2,1)S(1)}, bf16[4,256,512]{2,1,0:T(8,128)(2,1)S(1)}, u32[]{:S(2)}, u32[]{:S(2)}) collective-permute-start(bf16[4,256,512]{2,1,0:T(8,128)(2,1)S(1)} %dynamic-slice_bitcast_fusion.1), channel_id=1, source_target_pairs={{0,4},{4,0},{8,12},{12,8},{16,20},{20,16},{24,28},{28,24},{1,5},{5... | collective-permute-start | bytes 3145736 | tf_op jit(solution)/shard_map/ppermute | solution.py:153
  189.5 8.2 %copy-start.5 = (bf16[2048,512]{1,0:T(8,128)(2,1)S(1)}, bf16[2048,512]{1,0:T(8,128)(2,1)}, u32[]{:S(2)}) copy-start(bf16[2048,512]{1,0:T(8,128)(2,1)} %convolution_convert_fusion.5) | copy-start | bytes 6291460
  191.3 22.9 %collective-permute-start.13 = (bf16[256,512]{1,0:T(8,128)(2,1)S(1)}, bf16[256,512]{1,0:T(8,128)(2,1)S(1)}, u32[]{:S(2)}, u32[]{:S(2)}) collective-permute-start(bf16[256,512]{1,0:T(8,128)(2,1)S(1)} %get-tuple-element.21), channel_id=1, source_target_pairs={{0,8},{4,12},{8,16},{12,20},{16,24},{20,28},{24,0},{28,4},{1,9},{5... | collective-permute-start | bytes 786440 | tf_op jit(solution)/shard_map/ppermute | solution.py:130
  195.3 25.1 %collective-permute-start.14 = (bf16[256,512]{1,0:T(8,128)(2,1)S(1)}, bf16[256,512]{1,0:T(8,128)(2,1)S(1)}, u32[]{:S(2)}, u32[]{:S(2)}) collective-permute-start(bf16[256,512]{1,0:T(8,128)(2,1)S(1)} %get-tuple-element.23), channel_id=1, source_target_pairs={{0,16},{4,20},{8,24},{12,28},{16,0},{20,4},{24,8},{28,12},{1,17},{... | collective-permute-start | bytes 786440 | tf_op jit(solution)/shard_map/ppermute | solution.py:130
  195.3 34.3 %collective-permute-start.15 = (bf16[256,512]{1,0:T(8,128)(2,1)S(1)}, bf16[256,512]{1,0:T(8,128)(2,1)S(1)}, u32[]{:S(2)}, u32[]{:S(2)}) collective-permute-start(bf16[256,512]{1,0:T(8,128)(2,1)S(1)} %get-tuple-element.22), channel_id=1, source_target_pairs={{0,24},{4,28},{8,0},{12,4},{16,8},{20,12},{24,16},{28,20},{1,25},{... | collective-permute-start | bytes 786440 | tf_op jit(solution)/shard_map/ppermute | solution.py:130
  200.0 33.6 %collective-permute-start.1 = (bf16[256,512]{1,0:T(8,128)(2,1)S(1)}, bf16[256,512]{1,0:T(8,128)(2,1)S(1)}, u32[]{:S(2)}, u32[]{:S(2)}) collective-permute-start(bf16[256,512]{1,0:T(8,128)(2,1)S(1)} %get-tuple-element.24), channel_id=1, source_target_pairs={{0,8},{4,12},{8,16},{12,20},{16,24},{20,28},{24,0},{28,4},{1,9},{5... | collective-permute-start | bytes 786440 | tf_op jit(solution)/shard_map/ppermute | solution.py:130
  210.9 33.9 %collective-permute-start.2 = (bf16[256,512]{1,0:T(8,128)(2,1)}, bf16[256,512]{1,0:T(8,128)(2,1)}, u32[]{:S(2)}, u32[]{:S(2)}) collective-permute-start(bf16[256,512]{1,0:T(8,128)(2,1)} %get-tuple-element.26), channel_id=1, source_target_pairs={{0,16},{4,20},{8,24},{12,28},{16,0},{20,4},{24,8},{28,12},{1,17},{... | collective-permute-start | bytes 786440 | tf_op jit(solution)/shard_map/ppermute | solution.py:130
  214.2 30.6 %collective-permute-start.3 = (bf16[256,512]{1,0:T(8,128)(2,1)S(1)}, bf16[256,512]{1,0:T(8,128)(2,1)}, u32[]{:S(2)}, u32[]{:S(2)}) collective-permute-start(bf16[256,512]{1,0:T(8,128)(2,1)S(1)} %get-tuple-element.25), channel_id=1, source_target_pairs={{0,24},{4,28},{8,0},{12,4},{16,8},{20,12},{24,16},{28,20},{1,25},{... | collective-permute-start | bytes 786440 | tf_op jit(solution)/shard_map/ppermute | solution.py:130
  220.4 25.6 %collective-permute-start.5 = (bf16[256,512]{1,0:T(8,128)(2,1)}, bf16[256,512]{1,0:T(8,128)(2,1)}, u32[]{:S(2)}, u32[]{:S(2)}) collective-permute-start(bf16[256,512]{1,0:T(8,128)(2,1)} %get-tuple-element.27), channel_id=1, source_target_pairs={{0,8},{4,12},{8,16},{12,20},{16,24},{20,28},{24,0},{28,4},{1,9},{5... | collective-permute-start | bytes 786440 | tf_op jit(solution)/shard_map/ppermute | solution.py:130
  229.6 26.5 %collective-permute-start.6 = (bf16[256,512]{1,0:T(8,128)(2,1)}, bf16[256,512]{1,0:T(8,128)(2,1)}, u32[]{:S(2)}, u32[]{:S(2)}) collective-permute-start(bf16[256,512]{1,0:T(8,128)(2,1)} %get-tuple-element.29), channel_id=1, source_target_pairs={{0,16},{4,20},{8,24},{12,28},{16,0},{20,4},{24,8},{28,12},{1,17},{... | collective-permute-start | bytes 786440 | tf_op jit(solution)/shard_map/ppermute | solution.py:130
  233.6 0.8 copy-start.9
  234.4 23.7 %collective-permute-start.7 = (bf16[256,512]{1,0:T(8,128)(2,1)}, bf16[256,512]{1,0:T(8,128)(2,1)}, u32[]{:S(2)}, u32[]{:S(2)}) collective-permute-start(bf16[256,512]{1,0:T(8,128)(2,1)} %get-tuple-element.28), channel_id=1, source_target_pairs={{0,24},{4,28},{8,0},{12,4},{16,8},{20,12},{24,16},{28,20},{1,25},{... | collective-permute-start | bytes 786440 | tf_op jit(solution)/shard_map/ppermute | solution.py:130
  259.3 5.8 %copy-start.1 = (bf16[2048,512]{1,0:T(8,128)(2,1)S(1)}, bf16[2048,512]{1,0:T(8,128)(2,1)}, u32[]{:S(2)}) copy-start(bf16[2048,512]{1,0:T(8,128)(2,1)} %param.14) | copy-start | bytes 6291460
Sparse Core Ops, SparseCore 0:
  9.6 25.2 all-gather.4
  36.4 22.5 all-gather.6
  60.6 22.5 all-gather.10
  88.3 22.5 all-gather.8
  124.8 31.4 reduce-scatter.4
  158.8 31.4 reduce-scatter.2

commit v2 on v1

--- a/solution.py
+++ b/solution.py
@@ -216,7 +216,9 @@
             rows, cols, (((0,), (0,)), ((), ())), preferred_element_type=jnp.float32
         ).astype(jnp.bfloat16)
     )
-    down_low = scatter_line_first(part(all_cot, hidden[:, :half]), patches)
+    quarter = half // 2
+    down_first = scatter_line_first(part(all_cot, hidden[:, :quarter]), patches)
+    down_low = scatter_pair_first(part(all_cot, hidden[:, quarter:half]), patches)
     down_high = scatter_pair_first(part(all_cot, hidden[:, half:]), patches)
     branch = lax.psum_scatter(
         jnp.dot(hidden, down_weight, preferred_element_type=jnp.float32).astype(jnp.bfloat16),
@@ -248,7 +250,7 @@
     )
     input_grad = (cotangent.astype(jnp.float32) + input_gradient).astype(jnp.bfloat16)
     up_grad = jnp.concatenate([up_low, up_high], axis=1)
-    down_grad = by_rows(jnp.concatenate([down_low, down_high], axis=1)).T
+    down_grad = by_rows(jnp.concatenate([down_first, down_low, down_high], axis=1)).T
     return (layer_output, input_grad, up_grad, down_grad)
 
 

time: 274 us -> 288 us (1.051)
  starting transfers between devices: 34.6 us -> 41 us
  local copies, waits for them, and re-layouts: 16.5 us -> 20.4 us
    ppermute x1, waiting for transfers between devices: 7.26 us -> 34.6 us  [scatter_line_first(): lax.ppermute(pick(pair, 1 - side).astype(jnp.bfloat16), 'patch', swap_pai...]
    ppermute x12 -> x15, waiting for transfers between devices: 52.6 us -> 27.3 us  [line_scatter(): lax.ppermute(pick(parts, lax.rem(place + shift, length)), 'patch', [(2 *...]
    ppermute x12 -> x15, starting transfers between devices: 29.6 us -> 34.1 us  [line_scatter(): lax.ppermute(pick(parts, lax.rem(place + shift, length)), 'patch', [(2 *...]
    unnamed x35 -> x45, local copies, waits for them, and re-layouts: 5.84 us -> 9.42 us
    dot_general x4 -> x5, matrix products: 9.89 us -> 9.28 us  [on_device(): lax.dot_general(rows, cols, (((0,), (0,)), ((), ())), preferred_element_t...]
    ppermute x3 -> x4, waiting for transfers between devices: 10.9 us -> 11.4 us  [scatter_pair_first(): lax.ppermute(theirs, 'patch', swap_pairs(patches))]
  transfers between devices with their start and end apart: 22 -> 26, of which waited for: 10 -> 10; matrix products, arithmetic and copies ran while one was open for 18% -> 17% of each run, Pallas kernels for 10% -> 9%
where the time goes in v2:
time: 288 us; the launch traced here: 285 us
  waiting for transfers between devices  107 us (37%)
  starting transfers between devices  41 us (14%)
  matrix products  34.1 us (12%)
  Pallas kernels  26.5 us (9%)
  blocking collectives  21.7 us (8%)
  local copies, waits for them, and re-layouts  20.4 us (7%)
  other arithmetic  19.3 us (7%)
  between operations  14.6 us (5%)
    ppermute x1, waiting for transfers between devices, scatter_line_first(): lax.ppermute(pick(pair, 1 - side).astype(jnp.bfloat16), 'patch', swap_pai...  34.6 us
    ppermute x15, starting transfers between devices, line_scatter(): lax.ppermute(pick(parts, lax.rem(place + shift, length)), 'patch', [(2 *...  34.1 us
    ppermute x15, waiting for transfers between devices, line_scatter(): lax.ppermute(pick(parts, lax.rem(place + shift, length)), 'patch', [(2 *...  27.3 us
    pallas_call x1, Pallas kernels, attend(): pl.pallas_call(attention_kernel, grid=(columns // head_width,), in_specs=...  26.5 us
    all_to_all x1, blocking collectives, on_device(): lax.all_to_all(packed, 'patch', split_axis=0, concat_axis=0, tiled=True)  21.7 us
    all_gather x1, waiting for transfers between devices, on_device(): obs_all = lax.all_gather(obs_rows, 'fsdp', axis=0, tiled=True)  16.3 us
    all_gather x1, waiting for transfers between devices, on_device(): lax.all_gather(assimilated_columns, 'fsdp', axis=1, tiled=True)  16 us
    ppermute x4, waiting for transfers between devices, scatter_pair_first(): lax.ppermute(theirs, 'patch', swap_pairs(patches))  11.4 us
  transfers between devices with their start and end apart: 26, of which 10 were waited for; matrix products, arithmetic and copies ran while one was open for 17% of the time, Pallas kernels for 9%

profile of v2, /device:TPU:0, one launch (start us, length us, event | category | flops | bytes accessed | tf_op | source)
XLA Modules:
  0.0 284.6 jit_solution(2469611094776747669)
XLA Ops:
  8.7 1.1 reduce-window.6
  10.0 0.8 fusion.44
  11.5 2.9 %scatter_custom_fusion = bf16[1024,256]{1,0:T(8,128)(2,1)S(1)} fusion(s32[512]{0:T(512)S(1)} %bitcast.129, bf16[512,256]{1,0:T(8,128)(2,1)} %param.10, bf16[]{:T(256)} %constant.153.clone.1), kind=kCustom, calls=%fused_computation.88 | custom fusion | bytes 524800 | tf_op jit(solution)/shard_map/scatter | solution.py:29
  14.4 21.7 %all_to_all.5 = bf16[8,128,256]{2,1,0:T(8,128)(2,1)} all-to-all(bf16[8,128,256]{2,1,0:T(8,128)(2,1)S(1)} %bitcast.125), channel_id=1, replica_groups=mesh['patch'=8,'fsdp'=4] {'patch'}, dimensions={0} | all-to-all | bytes 1048576 | tf_op jit(solution)/shard_map/all_to_all | solution.py:187
  36.9 1.1 constant_dynamic-slice_fusion.1
  38.0 1.1 constant_dynamic-slice_fusion.grid_ref
  39.1 3.6 %convolution_convert_fusion.7.q_ref = bf16[512,512]{1,0:T(8,128)(2,1)} fusion(bf16[512,2048]{1,0:T(8,128)(2,1)} %all-gather.5.cloned.1.call-done, bf16[2048,512]{1,0:T(8,128)(2,1)S(1)} %copy-done), kind=kOutput, calls=%fused_computation.34 | convolution fusion | flops 1074003968 | bytes 4718592 | tf_op jit(solution)/shard_map/dot_general | solution.py:190
  42.8 16.3 %all-gather.7.cloned.1.call-done.obs_ref = bf16[4096,256]{1,0:T(8,128)(2,1)} async-done(((bf16[1024,256]{1,0:T(8,128)(2,1)}), bf16[4096,256]{1,0:T(8,128)(2,1)}) %all-gather.7.cloned.1.call-update) | async-done | bytes 2097168 | tf_op jit(solution)/shard_map/all_gather | solution.py:189
  59.1 1.6 copy-done.2
  60.7 1.0 copy-done.3
  61.7 26.5 %shard_map.129 = bf16[512,512]{1,0:T(8,128)(2,1)} custom-call(bf16[512,512]{1,0:T(8,128)(2,1)S(1)} %copy-done.3, bf16[4096,256]{1,0:T(8,128)(2,1)S(1)} %copy-done.2, bf16[256,512]{1,0:T(8,128)(2,1)S(1)} %get-tuple-element.34.wk_ref, bf16[256,512]{1,0:T(8,128)(2,1)S(1)} %get-tuple-element.33.wv_ref, bf16[512,512]{1,0:T(8,128)(2,1)S(1)} %constant_dynamic-slice_fusion.grid_ref), custom_call_target="tpu_custom_call" | custom-call | flops 8589934592 | bytes 4194304 | tf_op jit(solution)/shard_map/pallas_call | solution.py:94
  88.5 6.5 %fusion.50 = f32[512,1024]{1,0:T(8,128)} fusion(bf16[512,2048]{1,0:T(8,128)(2,1)} %all-gather.11.cloned.1.call-done, bf16[1024,2048]{1,0:T(8,128)(2,1)} %param.18), kind=kOutput, calls=%fused_computation.110 | convolution fusion | flops 2147483648 | bytes 8388608 | tf_op jit(solution)/shard_map/dot_general | solution.py:230
  95.0 16.0 %all-gather.9.cloned.1.call-done = bf16[512,2048]{1,0:T(8,128)(2,1)} async-done(((bf16[512,512]{1,0:T(8,128)(2,1)}), bf16[512,2048]{1,0:T(8,128)(2,1)}) %all-gather.9.cloned.1.call-update) | async-done | bytes 2097168 | tf_op jit(solution)/shard_map/all_gather | solution.py:200
  111.0 2.1 convert_reduce_fusion
  113.9 7.2 %fusion.11 = (bf16[512,1024]{1,0:T(8,128)(2,1)S(1)}, bf16[512,1024]{1,0:T(8,128)(2,1)}) fusion(f32[512,1024]{1,0:T(8,128)S(1)} %copy-done.19, bf16[2048,1024]{1,0:T(8,128)(2,1)} %param.17, bf16[512,2048]{1,0:T(8,128)(2,1)S(1)} %copy-done.4, f32[2048]{0:T(1024)S(1)} %copy-done.16, f32[512]{0:T(512)S(1)} %add_rsqrt_fusion, f32[512]{0:T(512)S(1)} %broadcast_multiply_fusion), kind=kOutput, calls=%fused_computation.23 | convolution fusion | flops 2164260864 | bytes 10498048 | tf_op jit(solution)/shard_map/dot_general | solution.py:209
  121.1 1.0 copy-done.20
  122.1 3.7 %convolution_convert_fusion = bf16[512,2048]{1,0:T(8,128)(2,1)} fusion(bf16[512,1024]{1,0:T(8,128)(2,1)S(1)} %get-tuple-element.16, bf16[2048,1024]{1,0:T(8,128)(2,1)S(1)} %copy-done.17), kind=kOutput, calls=%fused_computation.10 | convolution fusion | flops 2148532224 | bytes 7340032 | tf_op jit(solution)/shard_map/dot_general | solution.py:238
  126.0 2.8 convolution_convert_fusion.6
  128.7 0.9 dynamic-slice_bitcast_fusion.9
  129.6 3.3 %collective-permute-start.10 = (bf16[2,256,256]{2,1,0:T(8,128)(2,1)}, bf16[2,256,256]{2,1,0:T(8,128)(2,1)}, u32[]{:S(2)}, u32[]{:S(2)}) collective-permute-start(bf16[2,256,256]{2,1,0:T(8,128)(2,1)} %get-tuple-element.19), channel_id=1, source_target_pairs={{0,24},{4,28},{8,0},{12,4},{16,8},{20,12},{24,16},{28,20},{1,25},{... | collective-permute-start | bytes 786440 | tf_op jit(solution)/shard_map/ppermute | solution.py:130
  132.9 1.1 collective-permute-start.9
  134.0 1.0 convolution_convert_fusion.5
  135.0 1.0 copy-done.6
  136.0 0.8 dynamic-slice_bitcast_fusion.3
  136.8 1.5 collective-permute-start.12
  138.3 1.3 convolution_convert_fusion.2
  139.6 1.1 dynamic-slice_bitcast_fusion
  141.6 1.6 convolution_convert_fusion.4
  143.3 1.4 copy-done.8
  144.6 1.0 dynamic-slice_bitcast_fusion.2
  145.7 3.7 %convolution_convert_fusion.1 = bf16[512,2048]{1,0:T(8,128)(2,1)} fusion(bf16[512,1024]{1,0:T(8,128)(2,1)S(1)} %copy-done.15, bf16[1024,2048]{1,0:T(8,128)(2,1)S(1)} %copy-done.18), kind=kOutput, calls=%fused_computation.11 | convolution fusion | flops 2148532224 | bytes 7340032 | tf_op jit(solution)/shard_map/dot_general | solution.py:224
  149.4 2.7 convolution_convert_fusion.3
  152.2 1.1 copy-done.13
  153.3 1.4 collective-permute-start
  154.7 1.4 collective-permute-done.9
  156.1 1.2 fusion.32
  157.4 1.5 collective-permute-start.11
  159.0 1.2 fusion.24
  160.2 1.1 collective-permute-start.13
  161.3 2.1 collective-permute-start.14
  163.4 34.6 %collective-permute-done.11 = bf16[256,256]{1,0:T(8,128)(2,1)S(1)} collective-permute-done((bf16[256,256]{1,0:T(8,128)(2,1)S(1)}, bf16[256,256]{1,0:T(8,128)(2,1)S(1)}, u32[]{:S(2)}, u32[]{:S(2)}) %collective-permute-start.11) | collective-permute-done | bytes 131104 | tf_op jit(solution)/shard_map/ppermute | solution.py:162
  198.0 3.0 %collective-permute-start.15 = (bf16[256,256]{1,0:T(8,128)(2,1)S(1)}, bf16[256,256]{1,0:T(8,128)(2,1)S(1)}, u32[]{:S(2)}, u32[]{:S(2)}) collective-permute-start(bf16[256,256]{1,0:T(8,128)(2,1)S(1)} %get-tuple-element.31), channel_id=1, source_target_pairs={{0,24},{4,28},{8,0},{12,4},{16,8},{20,12},{24,16},{28,20},{1,25},{... | collective-permute-start | bytes 393224 | tf_op jit(solution)/shard_map/ppermute | solution.py:130
  201.1 1.5 collective-permute-start.4
  202.6 1.6 collective-permute-done.15
  204.3 1.7 fusion.12
  206.1 2.1 collective-permute-start.17
  208.2 2.1 collective-permute-start.18
  211.7 1.7 collective-permute-start.1
  213.3 11.4 %collective-permute-done.4 = bf16[4,256,512]{2,1,0:T(8,128)(2,1)S(1)} collective-permute-done((bf16[4,256,512]{2,1,0:T(8,128)(2,1)S(1)}, bf16[4,256,512]{2,1,0:T(8,128)(2,1)S(1)}, u32[]{:S(2)}, u32[]{:S(2)}) %collective-permute-start.4) | collective-permute-done | bytes 1048608 | tf_op jit(solution)/shard_map/ppermute | solution.py:153
  224.7 1.4 collective-permute-start.2
  226.4 0.9 dynamic-slice_bitcast_fusion.12
  227.3 1.2 collective-permute-start.3
  228.5 4.5 %collective-permute-done.18 = bf16[256,512]{1,0:T(8,128)(2,1)S(1)} collective-permute-done((bf16[256,512]{1,0:T(8,128)(2,1)S(1)}, bf16[256,512]{1,0:T(8,128)(2,1)S(1)}, u32[]{:S(2)}, u32[]{:S(2)}) %collective-permute-start.18) | collective-permute-done | bytes 262176 | tf_op jit(solution)/shard_map/ppermute | solution.py:130
  233.0 8.0 %collective-permute-start.5 = (bf16[256,512]{1,0:T(8,128)(2,1)}, bf16[256,512]{1,0:T(8,128)(2,1)}, u32[]{:S(2)}, u32[]{:S(2)}) collective-permute-start(bf16[256,512]{1,0:T(8,128)(2,1)} %get-tuple-element.27), channel_id=1, source_target_pairs={{0,8},{4,12},{8,16},{12,20},{16,24},{20,28},{24,0},{28,4},{1,9},{5... | collective-permute-start | bytes 786440 | tf_op jit(solution)/shard_map/ppermute | solution.py:130
  241.1 3.9 %collective-permute-start.6 = (bf16[256,512]{1,0:T(8,128)(2,1)}, bf16[256,512]{1,0:T(8,128)(2,1)}, u32[]{:S(2)}, u32[]{:S(2)}) collective-permute-start(bf16[256,512]{1,0:T(8,128)(2,1)} %get-tuple-element.29), channel_id=1, source_target_pairs={{0,16},{4,20},{8,24},{12,28},{16,0},{20,4},{24,8},{28,12},{1,17},{... | collective-permute-start | bytes 786440 | tf_op jit(solution)/shard_map/ppermute | solution.py:130
  245.8 2.8 collective-permute-start.7
  248.7 1.3 copy.21
  250.0 8.9 %collective-permute-done.2 = bf16[256,512]{1,0:T(8,128)(2,1)} collective-permute-done((bf16[256,512]{1,0:T(8,128)(2,1)}, bf16[256,512]{1,0:T(8,128)(2,1)}, u32[]{:S(2)}, u32[]{:S(2)}) %collective-permute-start.2) | collective-permute-done | bytes 262176 | tf_op jit(solution)/shard_map/ppermute | solution.py:130
  258.9 1.2 fusion.36
  260.2 10.0 %collective-permute-done.6 = bf16[256,512]{1,0:T(8,128)(2,1)} collective-permute-done((bf16[256,512]{1,0:T(8,128)(2,1)}, bf16[256,512]{1,0:T(8,128)(2,1)}, u32[]{:S(2)}, u32[]{:S(2)}) %collective-permute-start.6) | collective-permute-done | bytes 262176 | tf_op jit(solution)/shard_map/ppermute | solution.py:130
  270.9 1.2 fusion.34
  272.1 1.1 pad_maximum_fusion
  273.2 1.6 fusion.25
  274.8 2.9 %fusion.23 = (bf16[128,2048]{1,0:T(8,128)(2,1)}, bf16[128,2048]{1,0:T(8,128)(2,1)}) fusion(bf16[128,2048]{1,0:T(8,128)(2,1)} %reduce-scatter.5.cloned.1.call-done, bf16[128,2048]{1,0:T(8,128)(2,1)S(1)} %copy-done.12, f32[128]{0:T(128)S(1)} %broadcast_multiply_fusion.1, f32[128]{0:T(128)S(1)} %broadcast_multiply_fusion.2, ...), kind=kLoop, calls=%fused_computation.43 | loop fusion | flops 3932160 | bytes 3155972 | tf_op jit(solution)/shard_map/convert_element_type | solution.py:251
  (94 shorter events, 9.0 us)
Async XLA Ops:
  7.2 32.0 %copy-start = (bf16[2048,512]{1,0:T(8,128)(2,1)S(1)}, bf16[2048,512]{1,0:T(8,128)(2,1)}, u32[]{:S(2)}) copy-start(bf16[2048,512]{1,0:T(8,128)(2,1)} %param.14) | copy-start | bytes 6291460
  7.2 30.8 %all-gather.5.cloned.1.call-start = ((), (), s32[]{:S(2)}) async-start(), calls=%async_computation.3 | async-start | bytes 2621440 | tf_op jit(solution)/shard_map/all_gather | solution.py:185
  7.9 51.2 %all-gather.7.cloned.1.call-start = ((), (), s32[]{:S(2)}) async-start(), calls=%async_computation.4 | async-start | bytes 2621440 | tf_op jit(solution)/shard_map/all_gather | solution.py:189
  36.1 52.3 %all-gather.11.cloned.1.call-start = ((), (), s32[]{:S(2)}) async-start(), calls=%async_computation.7 | async-start | bytes 2621440 | tf_op jit(solution)/shard_map/all_gather | solution.py:211
  36.9 74.1 %all-gather.9.cloned.1.call-start = ((), (), s32[]{:S(2)}) async-start(), calls=%async_computation.5 | async-start | bytes 2621440 | tf_op jit(solution)/shard_map/all_gather | solution.py:200
  59.1 1.6 copy-start.2
  60.7 1.0 copy-start.3
  88.2 185.0 %reduce-scatter.5.cloned.1.call-start = ((), (), s32[]{:S(2)}) async-start(), calls=%async_computation.8 | async-start | bytes 2621440 | tf_op jit(solution)/shard_map/reduce_scatter | solution.py:237
  111.0 2.2 copy-start.4
  111.0 2.9 %copy-start.16 = (f32[2048]{0:T(1024)S(1)}, f32[2048]{0:T(1024)}, u32[]{:S(2)}) copy-start(f32[2048]{0:T(1024)} %param.13) | copy-start | bytes 24580
  111.0 2.9 %copy-start.19 = (f32[512,1024]{1,0:T(8,128)S(1)}, f32[512,1024]{1,0:T(8,128)}, u32[]{:S(2)}) copy-start(f32[512,1024]{1,0:T(8,128)} %fusion.50) | copy-start | bytes 6291460
  113.9 8.2 %copy-start.17 = (bf16[2048,1024]{1,0:T(8,128)(2,1)S(1)}, bf16[2048,1024]{1,0:T(8,128)(2,1)}, u32[]{:S(2)}) copy-start(bf16[2048,1024]{1,0:T(8,128)(2,1)} %param.17) | copy-start | bytes 12582916
  121.1 1.0 copy-start.20
  125.8 148.9 %reduce-scatter.3.cloned.1.call-start = ((), (), s32[]{:S(2)}) async-start(), calls=%async_computation.6 | async-start | bytes 2621440 | tf_op jit(solution)/shard_map/reduce_scatter | solution.py:223
  126.0 8.1 %copy-start.5 = (bf16[512,2048]{1,0:T(8,128)(2,1)S(1)}, bf16[512,2048]{1,0:T(8,128)(2,1)}, u32[]{:S(2)}) copy-start(bf16[512,2048]{1,0:T(8,128)(2,1)} %all-gather.11.cloned.1.call-done) | copy-start | bytes 6291460
  126.0 8.1 %copy-start.15 = (bf16[512,1024]{1,0:T(8,128)(2,1)S(1)}, bf16[512,1024]{1,0:T(8,128)(2,1)}, u32[]{:S(2)}) copy-start(bf16[512,1024]{1,0:T(8,128)(2,1)} %get-tuple-element.17) | copy-start | bytes 3145732
  129.6 22.6 %collective-permute-start.10 = (bf16[2,256,256]{2,1,0:T(8,128)(2,1)}, bf16[2,256,256]{2,1,0:T(8,128)(2,1)}, u32[]{:S(2)}, u32[]{:S(2)}) collective-permute-start(bf16[2,256,256]{2,1,0:T(8,128)(2,1)} %get-tuple-element.19), channel_id=1, source_target_pairs={{0,24},{4,28},{8,0},{12,4},{16,8},{20,12},{24,16},{28,20},{1,25},{... | collective-permute-start | bytes 786440 | tf_op jit(solution)/shard_map/ppermute | solution.py:130
  132.9 21.8 %collective-permute-start.8 = (bf16[2,256,256]{2,1,0:T(8,128)(2,1)}, bf16[2,256,256]{2,1,0:T(8,128)(2,1)}, u32[]{:S(2)}, u32[]{:S(2)}) collective-permute-start(bf16[2,256,256]{2,1,0:T(8,128)(2,1)} %get-tuple-element.18), channel_id=1, source_target_pairs={{0,8},{4,12},{8,16},{12,20},{16,24},{20,28},{24,0},{28,4},{1,9},{5... | collective-permute-start | bytes 786440 | tf_op jit(solution)/shard_map/ppermute | solution.py:130
  132.9 23.2 %collective-permute-start.9 = (bf16[2,256,256]{2,1,0:T(8,128)(2,1)S(1)}, bf16[2,256,256]{2,1,0:T(8,128)(2,1)}, u32[]{:S(2)}, u32[]{:S(2)}) collective-permute-start(bf16[2,256,256]{2,1,0:T(8,128)(2,1)S(1)} %get-tuple-element.20), channel_id=1, source_target_pairs={{0,16},{4,20},{8,24},{12,28},{16,0},{20,4},{24,8},{28,12},{1,17},{... | collective-permute-start | bytes 786440 | tf_op jit(solution)/shard_map/ppermute | solution.py:130
  135.0 1.0 copy-start.6
  136.8 22.1 %collective-permute-start.12 = (bf16[4,256,256]{2,1,0:T(8,128)(2,1)}, bf16[4,256,256]{2,1,0:T(8,128)(2,1)}, u32[]{:S(2)}, u32[]{:S(2)}) collective-permute-start(bf16[4,256,256]{2,1,0:T(8,128)(2,1)} %dynamic-slice_bitcast_fusion.3), channel_id=1, source_target_pairs={{0,4},{4,0},{8,12},{12,8},{16,20},{20,16},{24,28},{28,24},{1,5},{5... | collective-permute-start | bytes 1572872 | tf_op jit(solution)/shard_map/ppermute | solution.py:153
  139.6 3.6 %copy-start.10 = (bf16[512,2048]{0,1:T(8,128)(2,1)}, bf16[512,2048]{0,1:T(8,128)(2,1)S(1)}, u32[]{:S(2)}) copy-start(bf16[512,2048]{0,1:T(8,128)(2,1)S(1)} %convolution_convert_fusion.2) | copy-start | bytes 6291460
  139.6 2.0 copy-start.21
  140.7 63.6 %collective-permute-start.16 = (bf16[4,256,512]{2,1,0:T(8,128)(2,1)}, bf16[4,256,512]{2,1,0:T(8,128)(2,1)}, u32[]{:S(2)}, u32[]{:S(2)}) collective-permute-start(bf16[4,256,512]{2,1,0:T(8,128)(2,1)} %dynamic-slice_bitcast_fusion), channel_id=1, source_target_pairs={{0,4},{4,0},{8,12},{12,8},{16,20},{20,16},{24,28},{28,24},{1,5},{5... | collective-permute-start | bytes 3145736 | tf_op jit(solution)/shard_map/ppermute | solution.py:153
  141.6 4.0 %copy-start.18 = (bf16[1024,2048]{1,0:T(8,128)(2,1)S(1)}, bf16[1024,2048]{1,0:T(8,128)(2,1)}, u32[]{:S(2)}) copy-start(bf16[1024,2048]{1,0:T(8,128)(2,1)} %param.18) | copy-start | bytes 12582916
  143.3 1.4 copy-start.8
  152.1 1.2 copy-start.13
  152.1 6.8 %copy-start.7 = (bf16[256,2048]{0,1:T(8,128)(2,1)S(1)}, bf16[256,2048]{0,1:T(8,128)(2,1)}, u32[]{:S(2)}) copy-start(bf16[256,2048]{0,1:T(8,128)(2,1)} %copy-done.6) | copy-start | bytes 3145732
  153.3 57.3 %collective-permute-start = (bf16[4,256,512]{2,1,0:T(8,128)(2,1)S(1)}, bf16[4,256,512]{2,1,0:T(8,128)(2,1)S(1)}, u32[]{:S(2)}, u32[]{:S(2)}) collective-permute-start(bf16[4,256,512]{2,1,0:T(8,128)(2,1)S(1)} %copy-done.13), channel_id=1, source_target_pairs={{0,4},{4,0},{8,12},{12,8},{16,20},{20,16},{24,28},{28,24},{1,5},{5... | collective-permute-start | bytes 3145736 | tf_op jit(solution)/shard_map/ppermute | solution.py:153
  157.4 47.0 %copy-start.11 = (bf16[512,2048]{0,1:T(8,128)(2,1)S(1)}, bf16[512,2048]{0,1:T(8,128)(2,1)}, u32[]{:S(2)}) copy-start(bf16[512,2048]{0,1:T(8,128)(2,1)} %copy-done.10) | copy-start | bytes 6291460
  157.4 40.6 %collective-permute-start.11 = (bf16[256,256]{1,0:T(8,128)(2,1)S(1)}, bf16[256,256]{1,0:T(8,128)(2,1)S(1)}, u32[]{:S(2)}, u32[]{:S(2)}) collective-permute-start(bf16[256,256]{1,0:T(8,128)(2,1)S(1)} %fusion.43), channel_id=1, source_target_pairs={{0,4},{4,0},{8,12},{12,8},{16,20},{20,16},{24,28},{28,24},{1,5},{5... | collective-permute-start | bytes 393224 | tf_op jit(solution)/shard_map/ppermute | solution.py:162
  160.2 40.9 %collective-permute-start.13 = (bf16[256,256]{1,0:T(8,128)(2,1)S(1)}, bf16[256,256]{1,0:T(8,128)(2,1)S(1)}, u32[]{:S(2)}, u32[]{:S(2)}) collective-permute-start(bf16[256,256]{1,0:T(8,128)(2,1)S(1)} %get-tuple-element.30), channel_id=1, source_target_pairs={{0,8},{4,12},{8,16},{12,20},{16,24},{20,28},{24,0},{28,4},{1,9},{5... | collective-permute-start | bytes 393224 | tf_op jit(solution)/shard_map/ppermute | solution.py:130
  161.3 41.3 %collective-permute-start.14 = (bf16[256,256]{1,0:T(8,128)(2,1)S(1)}, bf16[256,256]{1,0:T(8,128)(2,1)S(1)}, u32[]{:S(2)}, u32[]{:S(2)}) collective-permute-start(bf16[256,256]{1,0:T(8,128)(2,1)S(1)} %get-tuple-element.32), channel_id=1, source_target_pairs={{0,16},{4,20},{8,24},{12,28},{16,0},{20,4},{24,8},{28,12},{1,17},{... | collective-permute-start | bytes 393224 | tf_op jit(solution)/shard_map/ppermute | solution.py:130
  198.0 6.2 %collective-permute-start.15 = (bf16[256,256]{1,0:T(8,128)(2,1)S(1)}, bf16[256,256]{1,0:T(8,128)(2,1)S(1)}, u32[]{:S(2)}, u32[]{:S(2)}) collective-permute-start(bf16[256,256]{1,0:T(8,128)(2,1)S(1)} %get-tuple-element.31), channel_id=1, source_target_pairs={{0,24},{4,28},{8,0},{12,4},{16,8},{20,12},{24,16},{28,20},{1,25},{... | collective-permute-start | bytes 393224 | tf_op jit(solution)/shard_map/ppermute | solution.py:130
  201.1 23.6 %collective-permute-start.4 = (bf16[4,256,512]{2,1,0:T(8,128)(2,1)S(1)}, bf16[4,256,512]{2,1,0:T(8,128)(2,1)S(1)}, u32[]{:S(2)}, u32[]{:S(2)}) collective-permute-start(bf16[4,256,512]{2,1,0:T(8,128)(2,1)S(1)} %dynamic-slice_bitcast_fusion.1), channel_id=1, source_target_pairs={{0,4},{4,0},{8,12},{12,8},{16,20},{20,16},{24,28},{28,24},{1,5},{5... | collective-permute-start | bytes 3145736 | tf_op jit(solution)/shard_map/ppermute | solution.py:153
  204.3 6.3 %copy-start.9 = (bf16[2048,512]{1,0:T(8,128)(2,1)S(1)}, bf16[2048,512]{1,0:T(8,128)(2,1)}, u32[]{:S(2)}) copy-start(bf16[2048,512]{1,0:T(8,128)(2,1)} %copy-done.8) | copy-start | bytes 6291460
  206.1 21.2 %collective-permute-start.17 = (bf16[256,512]{1,0:T(8,128)(2,1)S(1)}, bf16[256,512]{1,0:T(8,128)(2,1)S(1)}, u32[]{:S(2)}, u32[]{:S(2)}) collective-permute-start(bf16[256,512]{1,0:T(8,128)(2,1)S(1)} %get-tuple-element.21), channel_id=1, source_target_pairs={{0,8},{4,12},{8,16},{12,20},{16,24},{20,28},{24,0},{28,4},{1,9},{5... | collective-permute-start | bytes 786440 | tf_op jit(solution)/shard_map/ppermute | solution.py:130
  208.2 24.9 %collective-permute-start.18 = (bf16[256,512]{1,0:T(8,128)(2,1)S(1)}, bf16[256,512]{1,0:T(8,128)(2,1)S(1)}, u32[]{:S(2)}, u32[]{:S(2)}) collective-permute-start(bf16[256,512]{1,0:T(8,128)(2,1)S(1)} %get-tuple-element.23), channel_id=1, source_target_pairs={{0,16},{4,20},{8,24},{12,28},{16,0},{20,4},{24,8},{28,12},{1,17},{... | collective-permute-start | bytes 786440 | tf_op jit(solution)/shard_map/ppermute | solution.py:130
  210.2 30.8 %collective-permute-start.19 = (bf16[256,512]{1,0:T(8,128)(2,1)S(1)}, bf16[256,512]{1,0:T(8,128)(2,1)S(1)}, u32[]{:S(2)}, u32[]{:S(2)}) collective-permute-start(bf16[256,512]{1,0:T(8,128)(2,1)S(1)} %get-tuple-element.22), channel_id=1, source_target_pairs={{0,24},{4,28},{8,0},{12,4},{16,8},{20,12},{24,16},{28,20},{1,25},{... | collective-permute-start | bytes 786440 | tf_op jit(solution)/shard_map/ppermute | solution.py:130
  211.7 33.4 %collective-permute-start.1 = (bf16[256,512]{1,0:T(8,128)(2,1)S(1)}, bf16[256,512]{1,0:T(8,128)(2,1)S(1)}, u32[]{:S(2)}, u32[]{:S(2)}) collective-permute-start(bf16[256,512]{1,0:T(8,128)(2,1)S(1)} %get-tuple-element.24), channel_id=1, source_target_pairs={{0,8},{4,12},{8,16},{12,20},{16,24},{20,28},{24,0},{28,4},{1,9},{5... | collective-permute-start | bytes 786440 | tf_op jit(solution)/shard_map/ppermute | solution.py:130
  224.7 34.2 %collective-permute-start.2 = (bf16[256,512]{1,0:T(8,128)(2,1)}, bf16[256,512]{1,0:T(8,128)(2,1)}, u32[]{:S(2)}, u32[]{:S(2)}) collective-permute-start(bf16[256,512]{1,0:T(8,128)(2,1)} %get-tuple-element.26), channel_id=1, source_target_pairs={{0,16},{4,20},{8,24},{12,28},{16,0},{20,4},{24,8},{28,12},{1,17},{... | collective-permute-start | bytes 786440 | tf_op jit(solution)/shard_map/ppermute | solution.py:130
  227.3 31.6 %collective-permute-start.3 = (bf16[256,512]{1,0:T(8,128)(2,1)S(1)}, bf16[256,512]{1,0:T(8,128)(2,1)}, u32[]{:S(2)}, u32[]{:S(2)}) collective-permute-start(bf16[256,512]{1,0:T(8,128)(2,1)S(1)} %get-tuple-element.25), channel_id=1, source_target_pairs={{0,24},{4,28},{8,0},{12,4},{16,8},{20,12},{24,16},{28,20},{1,25},{... | collective-permute-start | bytes 786440 | tf_op jit(solution)/shard_map/ppermute | solution.py:130
  233.0 27.1 %collective-permute-start.5 = (bf16[256,512]{1,0:T(8,128)(2,1)}, bf16[256,512]{1,0:T(8,128)(2,1)}, u32[]{:S(2)}, u32[]{:S(2)}) collective-permute-start(bf16[256,512]{1,0:T(8,128)(2,1)} %get-tuple-element.27), channel_id=1, source_target_pairs={{0,8},{4,12},{8,16},{12,20},{16,24},{20,28},{24,0},{28,4},{1,9},{5... | collective-permute-start | bytes 786440 | tf_op jit(solution)/shard_map/ppermute | solution.py:130
  241.1 29.1 %collective-permute-start.6 = (bf16[256,512]{1,0:T(8,128)(2,1)}, bf16[256,512]{1,0:T(8,128)(2,1)}, u32[]{:S(2)}, u32[]{:S(2)}) collective-permute-start(bf16[256,512]{1,0:T(8,128)(2,1)} %get-tuple-element.29), channel_id=1, source_target_pairs={{0,16},{4,20},{8,24},{12,28},{16,0},{20,4},{24,8},{28,12},{1,17},{... | collective-permute-start | bytes 786440 | tf_op jit(solution)/shard_map/ppermute | solution.py:130
  245.1 0.7 copy-start.14
  245.8 25.1 %collective-permute-start.7 = (bf16[256,512]{1,0:T(8,128)(2,1)}, bf16[256,512]{1,0:T(8,128)(2,1)}, u32[]{:S(2)}, u32[]{:S(2)}) collective-permute-start(bf16[256,512]{1,0:T(8,128)(2,1)} %get-tuple-element.28), channel_id=1, source_target_pairs={{0,24},{4,28},{8,0},{12,4},{16,8},{20,12},{24,16},{28,20},{1,25},{... | collective-permute-start | bytes 786440 | tf_op jit(solution)/shard_map/ppermute | solution.py:130
  260.2 14.6 %copy-start.12 = (bf16[128,2048]{1,0:T(8,128)(2,1)S(1)}, bf16[128,2048]{1,0:T(8,128)(2,1)}, u32[]{:S(2)}) copy-start(bf16[128,2048]{1,0:T(8,128)(2,1)} %param.19) | copy-start | bytes 1572868
  272.1 5.6 %copy-start.1 = (bf16[2048,512]{1,0:T(8,128)(2,1)S(1)}, bf16[2048,512]{1,0:T(8,128)(2,1)}, u32[]{:S(2)}) copy-start(bf16[2048,512]{1,0:T(8,128)(2,1)} %param.14) | copy-start | bytes 6291460
Sparse Core Ops, SparseCore 0:
  9.6 25.2 all-gather.4
  36.4 22.5 all-gather.6
  60.6 22.5 all-gather.10
  88.3 22.5 all-gather.8
  126.0 31.4 reduce-scatter.4
  160.0 31.4 reduce-scatter.2
